TPU v7x, 256 devices: a whole 4x4x8 slice. The times are simulated.
256 devices in a mesh: member: 32 (over z, x), tile: 8 (over y, core).
Axes of the slice: x: 4, y: 4, z: 8, core: 2. Of those that a mesh axis runs over, the one named last changes fastest.
Arguments:
- background: bfloat16 [256, 80, 64, 512], P('member', None, 'tile'), may hold values from -6 to 6
- obs_cell: int32 [32, 8, 256], P('member', 'tile'), may hold values from 0 to 127
- obs_channel: int32 [32, 8, 256], P('member', 'tile'), may hold values from 0 to 79
- obs_count: int32 [32, 8], P('member', 'tile'), may hold values from 1 to 256, as said below
- obs_value: float32 [32, 8, 256], P('member', 'tile'), may hold values from -8 to 8
- obs_precision: float32 [32, 8, 256], P('member', 'tile'), may hold values from 0.25 to 4
Outputs:
- analysis: bfloat16 [256, 80, 64, 512], P('member', None, 'tile')
Inputs may be any that keep to these rules, and one draw needn't show every extreme that they name: obs_count is uneven across tiles; some tile has all 256 slots live.
All inputs are finite; a program needn't handle non-finite values.
Results may differ from a plain program's by a relative error of at most 0.0051.
Values may be sent and summed in bfloat16 or wider, within the bound.
No kernel may reach another device: no remote copies, remote signals or barrier semaphores. Data moves between devices by JAX's collectives and lax.ppermute only.
A program may use at most 192 MiB of HBM per device.

v0:
```python
import jax
import jax.numpy as jnp
from jax import lax
from jax.sharding import PartitionSpec as P

LAT_DEV = 8
LON_DEV = 16
PATCH_LAT = 4
NS_ITERS = 6
LOC = 8


def with_halo(cells, sides, width, closed):
    for axis, dim in sides:
        count = lax.axis_size(axis)
        ends = count if closed else count - 1
        head = lax.slice_in_dim(cells, 0, width, axis=dim)
        tail = lax.slice_in_dim(cells, cells.shape[dim] - width, cells.shape[dim], axis=dim)
        cells = jnp.concatenate(
            [
                lax.ppermute(tail, axis, [(i, (i + 1) % count) for i in range(ends)]),
                cells,
                lax.ppermute(head, axis, [((i + 1) % count, i) for i in range(ends)]),
            ],
            axis=dim,
        )
    return cells


def obs_pack(values, obs_value, obs_precision, obs_count, obs_cell):
    members = values.astype(jnp.float32)
    centre = jnp.mean(members, axis=0)
    anomaly = members - centre[None]
    departure = obs_value - centre
    slot_index = jnp.arange(values.shape[1], dtype=jnp.int32)
    inside = (slot_index < obs_count).astype(jnp.float32)
    weight = inside * obs_precision / (values.shape[0] - 1.0)
    row_pos = (obs_cell // LON_DEV).astype(jnp.float32)
    col_pos = (obs_cell % LON_DEV).astype(jnp.float32)
    return jnp.concatenate(
        [anomaly, departure[None], weight[None], row_pos[None], col_pos[None]], 0
    )


def tile_weights(nearby):
    members = nearby.shape[2] - 4
    highest = lax.Precision.HIGHEST
    shifts = jnp.arange(3, dtype=jnp.float32) - 1.0
    lat_pos = nearby[:, :, members + 2, :] + (shifts * LAT_DEV)[None, :, None]
    lon_pos = nearby[:, :, members + 3, :] + (shifts * LON_DEV)[:, None, None]
    patch_count = LAT_DEV // PATCH_LAT
    lat_centre = jnp.arange(patch_count, dtype=jnp.float32) * PATCH_LAT + (PATCH_LAT - 1) / 2.0
    lon_centre = (LON_DEV - 1) / 2.0
    dist = (lat_pos[None] - lat_centre[:, None, None, None]) ** 2 + (
        lon_pos[None] - lon_centre
    ) ** 2
    taper = jnp.exp(-dist / (2.0 * LOC * LOC))
    obs_weight = (taper * nearby[:, :, members + 1, :][None]).reshape(patch_count, -1)
    anomaly = nearby[:, :, :members, :].transpose(2, 0, 1, 3).reshape(members, -1)
    departure = nearby[:, :, members, :].reshape(-1)
    gram = jnp.einsum("ko,po,jo->pkj", anomaly, obs_weight, anomaly, precision=highest)
    drive = jnp.einsum("ko,po->pk", anomaly, obs_weight * departure[None], precision=highest)
    identity = jnp.eye(members, dtype=jnp.float32)
    system = identity[None] + gram
    scale = jnp.sqrt(jnp.sum(system * system, axis=(1, 2)))
    root = system / scale[:, None, None]
    inverse = jnp.broadcast_to(identity, system.shape)
    for sweep_index in range(NS_ITERS):
        factor = 1.5 * identity - 0.5 * jnp.matmul(inverse, root, precision=highest)
        root = jnp.matmul(root, factor, precision=highest)
        inverse = jnp.matmul(factor, inverse, precision=highest)
    spread = inverse / jnp.sqrt(scale)[:, None, None]
    partial_w = jnp.einsum("pjk,pk->pj", spread, drive, precision=highest)
    shift = jnp.einsum("pjk,pk->pj", spread, partial_w, precision=highest)
    weights = (spread + shift[:, :, None]).astype(jnp.bfloat16)
    colsum = jnp.sum(weights.astype(jnp.float32), axis=1)
    return (weights, colsum)


def transform(states, weights, colsum):
    members, chans = (states.shape[0], states.shape[1])
    patch_count = weights.shape[0]
    mean_state = jnp.sum(states, axis=0, dtype=jnp.float32) / members
    blocked = states.reshape(members, chans, patch_count, PATCH_LAT, LON_DEV)
    mixed = jnp.einsum("jcpis,pjk->kcpis", blocked, weights, preferred_element_type=jnp.float32)
    mean_block = mean_state.reshape(chans, patch_count, PATCH_LAT, LON_DEV)
    keep = (1.0 - colsum).transpose(1, 0)[:, None, :, None, None]
    result = mixed + mean_block[None] * keep
    return result.astype(jnp.bfloat16).reshape(states.shape)


def per_device(background, obs_cell, obs_channel, obs_count, obs_value, obs_precision):
    own_cell = obs_cell[0, 0]
    own_channel = obs_channel[0, 0]
    states = lax.all_to_all(background, "member", split_axis=3, concat_axis=0, tiled=True)
    flat_states = states.reshape(states.shape[0], -1)
    values = jnp.take(flat_states, own_channel * (LAT_DEV * LON_DEV) + own_cell, axis=1)
    pack = obs_pack(values, obs_value[0, 0], obs_precision[0, 0], obs_count[0, 0], own_cell)[
        None, None
    ]
    lat_rows = with_halo(pack, (("tile", 1),), 1, False)
    nearby = with_halo(lat_rows, (("member", 0),), 1, True)
    weights, colsum = tile_weights(nearby)
    return lax.all_to_all(
        transform(states, weights, colsum), "member", split_axis=0, concat_axis=3, tiled=True
    )


def solution(mesh):
    in_specs = (
        P("member", None, "tile", None),
        P("member", "tile", None),
        P("member", "tile", None),
        P("member", "tile"),
        P("member", "tile", None),
        P("member", "tile", None),
    )
    out_specs = P("member", None, "tile", None)
    return jax.shard_map(
        per_device, mesh=mesh, in_specs=in_specs, out_specs=out_specs, check_vma=False
    )
```

profile of v0, /device:TPU:8, one launch (start us, length us, event | category | flops | bytes accessed | tf_op | source)
XLA Modules:
  0.0 648.4 jit_solution(1748425051968770954)
XLA Ops:
  0.0 12.3 %copy.50 = bf16[8,80,8,512]{1,2,0,3:T(8,128)(2,1)} copy(bf16[8,80,8,512]{3,2,1,0:T(8,128)(2,1)} %param.6) | data formatting | bytes 10485760 | tf_op args[0]
  12.3 11.6 %all-to-all-start = ((bf16[8,80,8,512]{1,2,0,3:T(8,128)(2,1)}), bf16[8,80,8,512]{1,2,0,3:T(8,128)(2,1)}, u32[]{:S(2)}, u32[]{:S(2)}) async-start(bf16[8,80,8,512]{1,2,0,3:T(8,128)(2,1)} %copy.50), calls=%async_computation | async-start | bytes 16777216 | tf_op jit(solution)/shard_map/all_to_all | solution.py:95
  23.9 0.0 copy-done.2
  23.9 0.1 copy.55
  24.1 0.1 copy.54
  24.9 0.1 fusion.23
  25.1 187.1 %all-to-all-done = bf16[8,80,8,512]{1,2,0,3:T(8,128)(2,1)} async-done(((bf16[8,80,8,512]{1,2,0,3:T(8,128)(2,1)}), bf16[8,80,8,512]{1,2,0,3:T(8,128)(2,1)}, u32[]{:S(2)}, u32[]{:S(2)}) %all-to-all-start) | async-done | bytes 5242912 | tf_op jit(solution)/shard_map/all_to_all | solution.py:95
  212.2 34.6 %copy.52 = bf16[32,8,80,8,16]{4,3,2,1,0:T(8,128)(2,1)} copy(bf16[32,8,80,8,16]{2,3,1,4,0:T(8,128)(2,1)} %bitcast.3) | data formatting | bytes 10485760 | tf_op jit(solution)/shard_map/all_to_all | solution.py:95
  246.9 74.0 %reshape.276 = bf16[256,10240]{1,0:T(8,128)(2,1)} reshape(bf16[32,8,80,8,16]{4,3,2,1,0:T(8,128)(2,1)} %copy.52) | data formatting | bytes 10485760 | tf_op jit(solution)/shard_map/reshape | solution.py:96
  320.9 7.9 %copy.53 = bf16[256,10240]{0,1:T(8,128)(2,1)} copy(bf16[256,10240]{1,0:T(8,128)(2,1)} %reshape.276) | data formatting | bytes 10485760 | tf_op jit(solution)/shard_map/reshape | solution.py:96
  328.8 4.1 gather_fusion
  332.9 0.2 convert_reduce_fusion.2
  333.1 0.1 fusion.15
  333.3 0.1 copy.59
  333.4 0.2 concatenate.9
  333.6 1.9 collective-permute-start
  335.5 3.6 collective-permute-start.1
  339.3 3.5 collective-permute-done
  342.7 1.8 collective-permute-done.1
  344.5 0.1 pad_maximum_fusion.1
  344.5 1.8 copy.60
  346.3 3.1 collective-permute-start.2
  349.4 6.8 %collective-permute-start.3 = (f32[1,3,260,256]{3,0,2,1:T(1,128)}, f32[1,3,260,256]{3,0,2,1:T(1,128)}, u32[]{:S(2)}, u32[]{:S(2)}) collective-permute-start(f32[1,3,260,256]{3,0,2,1:T(1,128)} %copy.60), channel_id=1, source_target_pairs={{8,0},{16,8},{24,16},{32,24},{40,32},{48,40},{56,48},{64,56},{72,6... | collective-permute-start | bytes 2396168 | tf_op jit(solution)/shard_map/ppermute | solution.py:23
  356.3 0.1 add.144
  356.4 0.1 add.148
  356.4 8.8 %copy.80 = bf16[32,8,80,8,16]{2,1,0,4,3:T(8,128)(2,1)} copy(bf16[32,8,80,8,16]{2,3,1,4,0:T(8,128)(2,1)} %bitcast.3) | data formatting | bytes 10485760 | tf_op jit(solution)/shard_map/reshape | solution.py:84
  365.3 12.0 %copy.51 = bf16[8,80,8,512]{1,3,2,0:T(8,128)(2,1)} copy(bf16[8,80,8,512]{1,2,0,3:T(8,128)(2,1)} %all-to-all-done) | data formatting | bytes 10485760 | tf_op jit(solution)/shard_map/all_to_all | solution.py:95
  377.2 5.0 convert_reduce_fusion
  382.3 0.0 collective-permute-done.2
  382.3 2.3 copy.62
  384.6 0.0 collective-permute-done.3
  384.6 2.3 copy.63
  386.8 1.3 pad_maximum_fusion
  388.2 0.2 slice.25
  388.4 2.3 slice_reduce_fusion
  390.7 2.1 copy.64
  392.9 0.1 fusion.35
  393.0 5.6 multiply_reduce_fusion
  398.6 0.7 fusion.14
  399.3 0.7 fusion.25
  400.0 0.6 fusion.17
  400.7 0.7 fusion.13
  401.3 0.7 fusion.37
  402.0 0.7 fusion.36
  402.7 0.7 fusion.12
  403.3 0.7 fusion.39
  404.0 0.7 fusion.38
  404.6 0.7 fusion.11
  405.3 0.7 fusion.41
  406.0 0.7 fusion.40
  406.6 0.9 fusion.10
  407.5 1.4 fusion.43
  409.0 0.7 fusion.42
  409.7 1.1 convolution_bitcast_fusion
  410.8 1.7 fusion.9
  412.5 0.7 convolution_divide_fusion
  413.2 0.5 fusion.31
  413.7 0.6 fusion.29
  414.3 0.2 convert_reduce_fusion.1
  414.4 7.5 %fusion = bf16[256,80,2,4,16]{0,1,4,3,2:T(8,128)(2,1)} fusion(f32[256,2]{0,1:T(2,128)S(1)} %subtract_bitcast_fusion, f32[80,2,4,16]{0,3,2,1:T(8,128)S(1)} %bitcast.112, bf16[256,80,2,4,16]{1,0,4,3,2:T(8,128)(2,1)} %bitcast.103, f32[2,256,256]{2,1,0:T(8,128)S(1)} %convolution_divide_fusion, f32[2,256]{1,0:T(2,128)S(1)} %bitcast.114), kind=kOutput, calls=%fused_computation.3 | convolution fusion | flops 1350303744 | bytes 11055104 | tf_op jit(solution)/shard_map/jcpis,pjk->kcpis/dot_general | solution.py:85
  422.0 11.3 %copy.68 = bf16[256,80,8,16]{1,3,2,0:T(8,128)(2,1)} copy(bf16[256,80,8,16]{0,1,3,2:T(8,128)(2,1)} %bitcast.107) | data formatting | bytes 10485760 | tf_op jit(solution)/shard_map/reshape | solution.py:89
  433.3 194.6 %all_to_all.33 = bf16[256,80,8,16]{1,3,2,0:T(8,128)(2,1)} all-to-all(bf16[256,80,8,16]{1,3,2,0:T(8,128)(2,1)} %copy.68), channel_id=1, replica_groups=mesh['member'=32,'tile'=8] {'member'}, dimensions={0} | all-to-all | bytes 10485760 | tf_op jit(solution)/shard_map/all_to_all | solution.py:104
  627.9 8.9 %copy.69 = bf16[8,80,8,32,16]{1,4,3,2,0:T(8,128)(2,1)} copy(bf16[8,80,8,32,16]{1,4,2,0,3:T(8,128)(2,1)} %bitcast.105) | data formatting | bytes 10485760 | tf_op jit(solution)/shard_map/all_to_all | solution.py:104
  636.9 11.1 %copy.70 = bf16[8,80,8,512]{3,2,1,0:T(8,128)(2,1)} copy(bf16[8,80,8,512]{1,3,2,0:T(8,128)(2,1)} %bitcast.106) | data formatting | bytes 10485760 | tf_op jit(solution)/shard_map/all_to_all | solution.py:104
  (35 shorter events, 0.3 us)
Async XLA Ops:
  12.3 11.6 %copy-start.2 = (s32[1,1,256]{2,1,0:T(1,128)S(1)}, s32[1,1,256]{2,1,0:T(1,128)}, u32[]{:S(2)}) copy-start(s32[1,1,256]{2,1,0:T(1,128)} %param.7) | copy-start | bytes 3076
  12.3 11.7 %copy-start.3 = (f32[1,1,256]{2,1,0:T(1,128)S(1)}, f32[1,1,256]{2,1,0:T(1,128)}, u32[]{:S(2)}) copy-start(f32[1,1,256]{2,1,0:T(1,128)} %param.11) | copy-start | bytes 3076
  12.3 12.6 %copy-start.5 = (s32[1,1,256]{2,1,0:T(1,128)S(1)}, s32[1,1,256]{2,1,0:T(1,128)}, u32[]{:S(2)}) copy-start(s32[1,1,256]{2,1,0:T(1,128)} %param.8) | copy-start | bytes 3076
  12.3 199.9 %all-to-all-start = ((bf16[8,80,8,512]{1,2,0,3:T(8,128)(2,1)}), bf16[8,80,8,512]{1,2,0,3:T(8,128)(2,1)}, u32[]{:S(2)}, u32[]{:S(2)}) async-start(bf16[8,80,8,512]{1,2,0,3:T(8,128)(2,1)} %copy.50), calls=%async_computation | async-start | bytes 16777216 | tf_op jit(solution)/shard_map/all_to_all | solution.py:95
  320.8 12.4 %copy-start.4 = (f32[1,1,256]{2,1,0:T(1,128)S(1)}, f32[1,1,256]{2,1,0:T(1,128)}, u32[]{:S(2)}) copy-start(f32[1,1,256]{2,1,0:T(1,128)} %param.10) | copy-start | bytes 3076
  333.6 9.1 %collective-permute-start = (f32[1,1,260,256]{2,3,1,0:T(8,128)S(1)}, f32[1,1,260,256]{2,3,1,0:T(8,128)S(1)}, u32[]{:S(2)}, u32[]{:S(2)}) collective-permute-start(f32[1,1,260,256]{2,3,1,0:T(8,128)S(1)} %bitcast.108), channel_id=1, source_target_pairs={{0,1},{1,2},{2,3},{3,4},{4,5},{5,6},{6,7},{8,9},{9,10},{10,11},{11... | collective-permute-start | bytes 798728 | tf_op jit(solution)/shard_map/ppermute | solution.py:21
  335.5 8.9 %collective-permute-start.1 = (f32[1,1,260,256]{2,3,1,0:T(8,128)S(1)}, f32[1,1,260,256]{2,3,1,0:T(8,128)S(1)}, u32[]{:S(2)}, u32[]{:S(2)}) collective-permute-start(f32[1,1,260,256]{2,3,1,0:T(8,128)S(1)} %bitcast.109), channel_id=1, source_target_pairs={{1,0},{2,1},{3,2},{4,3},{5,4},{6,5},{7,6},{9,8},{10,9},{11,10},{12... | collective-permute-start | bytes 798728 | tf_op jit(solution)/shard_map/ppermute | solution.py:23
  342.7 22.5 %copy-start = (f32[1,1,260,256]{2,3,1,0:T(8,128)}, f32[1,1,260,256]{2,3,1,0:T(8,128)S(1)}, u32[]{:S(2)}) copy-start(f32[1,1,260,256]{2,3,1,0:T(8,128)S(1)} %collective-permute-done) | copy-start | bytes 798724
  344.5 20.8 %copy-start.1 = (f32[1,1,260,256]{2,3,1,0:T(8,128)}, f32[1,1,260,256]{2,3,1,0:T(8,128)S(1)}, u32[]{:S(2)}) copy-start(f32[1,1,260,256]{2,3,1,0:T(8,128)S(1)} %collective-permute-done.1) | copy-start | bytes 798724
  346.3 35.9 %collective-permute-start.2 = (f32[1,3,260,256]{3,0,2,1:T(1,128)}, f32[1,3,260,256]{3,0,2,1:T(1,128)}, u32[]{:S(2)}, u32[]{:S(2)}) collective-permute-start(f32[1,3,260,256]{3,0,2,1:T(1,128)} %copy.60), channel_id=1, source_target_pairs={{0,8},{8,16},{16,24},{24,32},{32,40},{40,48},{48,56},{56,64},{64,7... | collective-permute-start | bytes 2396168 | tf_op jit(solution)/shard_map/ppermute | solution.py:21
  349.4 35.1 %collective-permute-start.3 = (f32[1,3,260,256]{3,0,2,1:T(1,128)}, f32[1,3,260,256]{3,0,2,1:T(1,128)}, u32[]{:S(2)}, u32[]{:S(2)}) collective-permute-start(f32[1,3,260,256]{3,0,2,1:T(1,128)} %copy.60), channel_id=1, source_target_pairs={{8,0},{16,8},{24,16},{32,24},{40,32},{48,40},{56,48},{64,56},{72,6... | collective-permute-start | bytes 2396168 | tf_op jit(solution)/shard_map/ppermute | solution.py:23
where the time goes:
time: 658 us; the launch traced here: 648 us
  local copies, waits for them, and re-layouts  197 us (30%)
  blocking collectives  195 us (30%)
  waiting for transfers between devices  192 us (29%)
  matrix products  28.7 us (4%)
  starting transfers between devices  27.1 us (4%)
  other arithmetic  7.29 us (1%)
    all_to_all x1, blocking collectives, per_device(): lax.all_to_all(transform(states, weights, colsum), 'member', split_axis=0...  195 us
    all_to_all x1, waiting for transfers between devices, per_device(): lax.all_to_all(background, 'member', split_axis=3, concat_axis=0, tiled=T...  187 us
    reshape x2, local copies, waits for them, and re-layouts, per_device(): flat_states = states.reshape(states.shape[0], -1)  81.9 us
    all_to_all x2, local copies, waits for them, and re-layouts, per_device(): lax.all_to_all(background, 'member', split_axis=3, concat_axis=0, tiled=T...  46.6 us
    all_to_all x2, local copies, waits for them, and re-layouts, per_device(): lax.all_to_all(transform(states, weights, colsum), 'member', split_axis=0...  20 us
  transfers between devices with their start and end apart: 5, of which 3 were waited for; matrix products, arithmetic and copies ran while one was open for 4% of the time, Pallas kernels for 0%

commit v1 on v0

v1 whole, which is shorter than its diff:
```python
import functools

import jax
import jax.numpy as jnp
from jax import lax
from jax.experimental import pallas as pl
from jax.experimental.pallas import tpu as pltpu
from jax.sharding import PartitionSpec as P

LAT_DEV = 8
LON_DEV = 16
PATCH_LAT = 4
NS_ITERS = 6
LOC = 8
MEM_DEV = 8
LANES = 128
CHUNKS = (20, 20)
NT = (((1,), (1,)), ((), ()))
NN = (((1,), (0,)), ((), ()))
VMEM_LIMIT = 48 * 1024 * 1024


def swap_groups(parts, sign):
    lane_group = lax.broadcasted_iota(jnp.int32, parts[0].shape, 1) // LON_DEV
    parts = list(parts)
    for step in (4, 2, 1):
        low = (lane_group & step) == 0
        for i in range(8):
            if i & step:
                continue
            a, b = parts[i], parts[i + step]
            parts[i] = jnp.where(low, a, pltpu.roll(b, step * LON_DEV, 1))
            parts[i + step] = jnp.where(low, pltpu.roll(a, LANES - step * LON_DEV, 1), b)
    return parts


def pack_kernel(per_step, x_ref, o_ref):
    def pair(b, carry):
        rows = []
        for e in range(2):
            cells = x_ref[:, b * 2 + e].astype(jnp.float32)
            rows.append(jnp.transpose(cells, (1, 0, 2)))
        halves = []
        for p in range(2):
            halves.append(
                swap_groups([rows[e][p * 4 + r] for e in range(2) for r in range(4)], 1)
            )
        for a in range(8):
            both = jnp.concatenate([halves[0][a], halves[1][a]], axis=0)
            o_ref[a, b] = both.astype(jnp.bfloat16)
        return carry

    lax.fori_loop(0, per_step, pair, 0)


def pack(background, first, count, per_step):
    base = first // per_step
    return pl.pallas_call(
        functools.partial(pack_kernel, per_step),
        out_shape=jax.ShapeDtypeStruct((32, count, 16, LANES), jnp.bfloat16),
        grid=(count // per_step, 4),
        in_specs=[
            pl.BlockSpec((MEM_DEV, 2 * per_step, 8, LANES), lambda i, g: (0, base + i, 0, g))
        ],
        out_specs=pl.BlockSpec((8, per_step, 16, LANES), lambda i, g: (g, i, 0, 0)),
        cost_estimate=pl.CostEstimate(
            flops=count * 65536 * 40, bytes_accessed=count * 262144, transcendentals=0
        ),
        name="pack",
    )(background)


def unpack_kernel(per_step, x_ref, *rest):
    o_ref = rest[-1]

    def pair(b, carry):
        both = [x_ref[a, b].astype(jnp.float32) for a in range(8)]
        rows = [[None] * 8, [None] * 8]
        for p in range(2):
            parts = swap_groups([both[a][p * 8 : (p + 1) * 8] for a in range(8)], -1)
            for e in range(2):
                for r in range(4):
                    rows[e][p * 4 + r] = parts[e * 4 + r]
        for e in range(2):
            cells = jnp.transpose(jnp.stack(rows[e], axis=0), (1, 0, 2))
            o_ref[:, b * 2 + e] = cells.astype(jnp.bfloat16)
        return carry

    lax.fori_loop(0, per_step, pair, 0)


def unpack(blocks, previous, first, count, per_step, shape):
    base = first // per_step
    in_specs = [pl.BlockSpec((8, per_step, 16, LANES), lambda i, g: (g, i, 0, 0))]
    operands = [blocks]
    aliases = {}
    if previous is not None:
        in_specs.append(pl.BlockSpec(memory_space=pl.ANY))
        operands.append(previous)
        aliases = {1: 0}
    return pl.pallas_call(
        functools.partial(unpack_kernel, per_step),
        out_shape=jax.ShapeDtypeStruct(shape, jnp.bfloat16),
        grid=(count // per_step, 4),
        in_specs=in_specs,
        out_specs=pl.BlockSpec(
            (MEM_DEV, 2 * per_step, 8, LANES), lambda i, g: (0, base + i, 0, g)
        ),
        input_output_aliases=aliases,
        cost_estimate=pl.CostEstimate(
            flops=count * 65536 * 40, bytes_accessed=count * 262144, transcendentals=0
        ),
        name="unpack",
    )(*operands)


def gather_kernel(counts, tiles, info_ref, *refs):
    blocks, o_ref, held = refs[: len(counts)], refs[-2], refs[-1]
    step = pl.program_id(0)
    lane_index = lax.broadcasted_iota(jnp.int32, (LANES, 256), 0)
    for t in range(tiles):
        a = step * tiles + t
        info = info_ref[a]
        cell = info[0:1].astype(jnp.int32)
        channel = info[1:2].astype(jnp.int32)
        lane = (channel & 1) * 64 + (cell & 63)
        group = (channel >> 1) * 2 + (cell >> 6)
        pick = (lane_index == lane).astype(jnp.float32).astype(jnp.bfloat16)
        total = jnp.zeros((MEM_DEV, 256), jnp.float32)
        first = 0
        for block, count in zip(blocks, counts):
            rows = block[t].reshape(count * 16, LANES)
            found = lax.dot_general(rows, pick, NN, preferred_element_type=jnp.float32)
            found = found.reshape(count * 2, MEM_DEV, 256)
            for g in range(count * 2):
                total = total + jnp.where(group == first * 2 + g, found[g], 0.0)
            first += count
        held[lax.rem(a + 1, 32), 0:8] = total
        held[a, 8:16] = total
        held[lax.rem(a + 31, 32), 16:24] = total

    @pl.when(step == 32 // tiles - 1)
    def _():
        o_ref[...] = held[...].astype(jnp.bfloat16)


def gather_obs(info, blocks):
    counts = tuple(b.shape[1] for b in blocks)
    tiles = 4
    return pl.pallas_call(
        functools.partial(gather_kernel, counts, tiles),
        out_shape=jax.ShapeDtypeStruct((32, 24, 256), jnp.bfloat16),
        grid=(32 // tiles,),
        in_specs=[pl.BlockSpec((32, 4, 256), lambda i: (0, 0, 0))]
        + [pl.BlockSpec((tiles, c, 16, LANES), lambda i: (i, 0, 0, 0)) for c in counts],
        out_specs=pl.BlockSpec((32, 24, 256), lambda i: (0, 0, 0)),
        scratch_shapes=[pltpu.VMEM((32, 24, 256), jnp.float32)],
        compiler_params=pltpu.CompilerParams(vmem_limit_bytes=VMEM_LIMIT),
        cost_estimate=pl.CostEstimate(
            flops=2 * 32 * 640 * 256 * 128, bytes_accessed=6 << 20, transcendentals=0
        ),
        name="gather_obs",
    )(info, *blocks)


def split(x):
    high = x.astype(jnp.bfloat16)
    return high, (x - high.astype(jnp.float32)).astype(jnp.bfloat16)


def product(a, b, dims):
    a_high, a_low = a if isinstance(a, tuple) else split(a)
    b_high, b_low = b if isinstance(b, tuple) else split(b)
    dot = functools.partial(
        lax.dot_general, dimension_numbers=dims, preferred_element_type=jnp.float32
    )
    return dot(a_high, b_high) + (dot(a_high, b_low) + dot(a_low, b_high))


def weights_kernel(own, below, above, own_info, below_info, above_info, w_ref, keep_ref, gram):
    members = 256
    row_id = lax.broadcasted_iota(jnp.int32, (members, members), 0)
    col_id = lax.broadcasted_iota(jnp.int32, (members, members), 1)
    identity = (row_id == col_id).astype(jnp.float32)
    drive = [jnp.zeros((8, members), jnp.float32) for _ in range(2)]
    first = True
    lon_centre = (LON_DEV - 1) / 2.0
    for j, (values, infos) in enumerate(
        ((below, below_info), (own, own_info), (above, above_info))
    ):
        lat_shift = (j - 1.0) * LAT_DEV
        for i in range(3):
            lon_shift = (i - 1.0) * LON_DEV
            hx = values[...].astype(jnp.float32).reshape(32, 3, MEM_DEV, 256)[:, i]
            hx = hx.reshape(members, 256)
            centre = jnp.sum(hx, axis=0, keepdims=True) * (1.0 / members)
            y = hx - centre
            y_parts = split(y)
            info = infos[i]
            cell = info[0:1].astype(jnp.int32)
            departure = info[2:3] - centre
            weight = info[3:4]
            lat = (cell >> 4).astype(jnp.float32) + lat_shift
            lon = (cell & 15).astype(jnp.float32) + lon_shift
            for p in range(2):
                lat_centre = p * PATCH_LAT + (PATCH_LAT - 1) / 2.0
                dist = (lat - lat_centre) ** 2 + (lon - lon_centre) ** 2
                obs_weight = jnp.exp(-dist / (2.0 * LOC * LOC)) * weight
                term = product(y * obs_weight, y_parts, NT)
                if first:
                    gram[p] = identity + term
                else:
                    gram[p] += term
                pull = jnp.broadcast_to(obs_weight * departure, (8, 256))
                drive[p] = drive[p] + product(pull, y_parts, NT)
            first = False
    roots, inverses, scales = [], [], []
    for p in range(2):
        system = gram[p]
        scale = jnp.sqrt(jnp.sum(jnp.sum(system * system, axis=0, keepdims=True), axis=1, keepdims=True))
        roots.append(system / scale)
        scales.append(scale)
    for step in range(NS_ITERS):
        for p in range(2):
            if step == 0:
                factor = 1.5 * identity - 0.5 * roots[p]
                f_parts = split(factor)
                roots[p] = product(roots[p], f_parts, NN)
                inverses_p = factor
                if len(inverses) < 2:
                    inverses.append(inverses_p)
            else:
                i_parts = split(inverses[p])
                r_parts = split(roots[p])
                factor = 1.5 * identity - 0.5 * product(i_parts, r_parts, NN)
                f_parts = split(factor)
                if step < NS_ITERS - 1:
                    roots[p] = product(r_parts, f_parts, NN)
                inverses[p] = product(f_parts, i_parts, NN)
    for p in range(2):
        spread = inverses[p] / jnp.sqrt(scales[p])
        s_parts = split(spread)
        shift = product(product(drive[p], s_parts, NT), s_parts, NT)
        weights = (spread + shift[0:1]).astype(jnp.bfloat16)
        w_ref[p] = weights
        total = jnp.sum(weights.astype(jnp.float32), axis=1, keepdims=True)
        keep_ref[p] = jnp.broadcast_to(1.0 - total, (members, LANES))


def tile_weights(values, infos):
    vmem = pl.BlockSpec(memory_space=pltpu.VMEM)
    return pl.pallas_call(
        weights_kernel,
        out_shape=(
            jax.ShapeDtypeStruct((2, 256, 256), jnp.bfloat16),
            jax.ShapeDtypeStruct((2, 256, LANES), jnp.float32),
        ),
        in_specs=[vmem] * 6,
        out_specs=(vmem, vmem),
        scratch_shapes=[pltpu.VMEM((2, 256, 256), jnp.float32)],
        compiler_params=pltpu.CompilerParams(vmem_limit_bytes=VMEM_LIMIT),
        cost_estimate=pl.CostEstimate(
            flops=2 * 160 * 256**3, bytes_accessed=3 << 20, transcendentals=0
        ),
        name="tile_weights",
    )(*values, *infos)


def transform_kernel(per_step, x_ref, w_ref, keep_ref, o_ref):
    for b in range(per_step):
        both = x_ref[:, b].astype(jnp.float32).reshape(32, 2, MEM_DEV, LANES)
        outs = []
        for p in range(2):
            states = both[:, p].reshape(256, LANES)
            mean = jnp.sum(states, axis=0, keepdims=True) * (1.0 / 256.0)
            mixed = lax.dot_general(
                w_ref[p], states.astype(jnp.bfloat16), NN, preferred_element_type=jnp.float32
            )
            result = mixed + keep_ref[p] * mean
            outs.append(result.reshape(32, 1, MEM_DEV, LANES))
        result = jnp.concatenate(outs, axis=1).reshape(32, 16, LANES)
        o_ref[:, b] = result.astype(jnp.bfloat16)


def transform(blocks, weights, keep, per_step):
    count = blocks.shape[1]
    spec = pl.BlockSpec((32, per_step, 16, LANES), lambda i: (0, i, 0, 0))
    return pl.pallas_call(
        functools.partial(transform_kernel, per_step),
        out_shape=jax.ShapeDtypeStruct(blocks.shape, jnp.bfloat16),
        grid=(count // per_step,),
        in_specs=[
            spec,
            pl.BlockSpec((2, 256, 256), lambda i: (0, 0, 0)),
            pl.BlockSpec((2, 256, LANES), lambda i: (0, 0, 0)),
        ],
        out_specs=spec,
        compiler_params=pltpu.CompilerParams(vmem_limit_bytes=VMEM_LIMIT),
        cost_estimate=pl.CostEstimate(
            flops=count * 4 * 256 * 256 * 128, bytes_accessed=count * 262144, transcendentals=0
        ),
        name="transform",
    )(blocks, weights, keep)


def exchange(blocks):
    return lax.all_to_all(blocks, "member", split_axis=0, concat_axis=0, tiled=True)


def per_device(background, obs_cell, obs_channel, obs_count, obs_value, obs_precision):
    firsts = [sum(CHUNKS[:n]) for n in range(len(CHUNKS))]
    slots = obs_cell.shape[-1]
    members = 256
    blocks = [pack(background, f, c, 5) for f, c in zip(firsts, CHUNKS)]
    arrived = [exchange(b) for b in blocks]

    inside = (jnp.arange(slots, dtype=jnp.int32) < obs_count[0, 0]).astype(jnp.float32)
    weight = inside * obs_precision[0, 0] / (members - 1.0)
    own = jnp.stack(
        [
            obs_cell[0, 0].astype(jnp.float32),
            obs_channel[0, 0].astype(jnp.float32),
            obs_value[0, 0],
            weight,
        ]
    )
    info = lax.all_gather(own, "member")
    hx = exchange(gather_obs(info, blocks))
    me = lax.axis_index("member")
    near = jnp.stack(
        [
            lax.dynamic_index_in_dim(info, lax.rem(me + d, 32), 0, keepdims=False)
            for d in (31, 0, 1)
        ]
    )
    bands = lax.axis_size("tile")
    up = [(i, i + 1) for i in range(bands - 1)]
    down = [(i + 1, i) for i in range(bands - 1)]
    values = (hx, lax.ppermute(hx, "tile", up), lax.ppermute(hx, "tile", down))
    infos = (near, lax.ppermute(near, "tile", up), lax.ppermute(near, "tile", down))
    weights, keep = tile_weights(values, infos)

    back = [exchange(transform(b, weights, keep, 2)) for b in arrived]
    out = None
    for b, f, c in zip(back, firsts, CHUNKS):
        out = unpack(b, out, f, c, 5, background.shape)
    return out


def solution(mesh):
    in_specs = (
        P("member", None, "tile", None),
        P("member", "tile", None),
        P("member", "tile", None),
        P("member", "tile"),
        P("member", "tile", None),
        P("member", "tile", None),
    )
    out_specs = P("member", None, "tile", None)
    return jax.shard_map(
        per_device, mesh=mesh, in_specs=in_specs, out_specs=out_specs, check_vma=False
    )
```

time: 658 us -> 363 us (0.55); the launches traced: 648 us -> 361 us
  local copies, waits for them, and re-layouts: 197 us -> 6.28 us
  Pallas kernels: 0 us -> 108 us
  waiting for transfers between devices: 192 us -> 97.7 us
  blocking collectives: 195 us -> 121 us
  matrix products: 28.7 us -> 0 us
  other arithmetic: 7.29 us -> 0.03 us
    all_to_all x1 -> x2, blocking collectives: 195 us -> 74.9 us  [exchange(): lax.all_to_all(blocks, 'member', split_axis=0, concat_axis=0, tiled=True)]
    pallas_call x0 -> x8, Pallas kernels: none -> 108 us  [the longest x2 41.6 us: unpack(): pl.pallas_call(functools.partial(unpack_kernel, per_step), out_shape=jax....]
    reshape x5 -> x0, local copies, waits for them, and re-layouts: 104 us -> none  [the longest x2 81.9 us: per_device(): flat_states = states.reshape(states.shape[0], -1)]
    all_to_all x1 -> x3, waiting for transfers between devices: 187 us -> 94.6 us  [exchange(): lax.all_to_all(blocks, 'member', split_axis=0, concat_axis=0, tiled=True)]
    all_to_all x4 -> x0, local copies, waits for them, and re-layouts: 66.6 us -> none  [the longest x2 46.6 us: per_device(): lax.all_to_all(background, 'member', split_axis=3, concat_axis=0, tiled=T...]
    all_gather x0 -> x1, blocking collectives: none -> 46.3 us  [per_device(): info = lax.all_gather(own, 'member')]
    dot_general x22 -> x0, matrix products: 28.7 us -> none  [the longest x1 7.53 us: transform(): jnp.einsum('jcpis,pjk->kcpis', blocked, weights, preferred_element_type=j...]
    all_to_all x1 -> x3, starting transfers between devices: 11.6 us -> 16.7 us  [exchange(): lax.all_to_all(blocks, 'member', split_axis=0, concat_axis=0, tiled=True)]
  transfers between devices with their start and end apart: 5 -> 7, of which waited for: 3 -> 4; matrix products, arithmetic and copies ran while one was open for 4% -> 0% of each run, Pallas kernels for 0% -> 11%
where the time goes in v1:
time: 363 us; the launch traced here: 361 us
  blocking collectives  121 us (33%)
  Pallas kernels  108 us (30%)
  waiting for transfers between devices  97.7 us (27%)
  starting transfers between devices  26.4 us (7%)
  local copies, waits for them, and re-layouts  6.28 us (2%)
    all_to_all x3, waiting for transfers between devices, exchange(): lax.all_to_all(blocks, 'member', split_axis=0, concat_axis=0, tiled=True)  94.6 us
    all_to_all x2, blocking collectives, exchange(): lax.all_to_all(blocks, 'member', split_axis=0, concat_axis=0, tiled=True)  74.9 us
    all_gather x1, blocking collectives, per_device(): info = lax.all_gather(own, 'member')  46.3 us
    pallas_call x2, Pallas kernels, unpack(): pl.pallas_call(functools.partial(unpack_kernel, per_step), out_shape=jax....  41.6 us
    pallas_call x2, Pallas kernels, pack(): pl.pallas_call(functools.partial(pack_kernel, per_step), out_shape=jax.Sh...  41.4 us
    all_to_all x3, starting transfers between devices, exchange(): lax.all_to_all(blocks, 'member', split_axis=0, concat_axis=0, tiled=True)  16.7 us
    pallas_call x1, Pallas kernels, tile_weights(): pl.pallas_call(weights_kernel, out_shape=(jax.ShapeDtypeStruct((2, 256, 2...  10.9 us
    pallas_call x1, Pallas kernels, gather_obs(): pl.pallas_call(functools.partial(gather_kernel, counts, tiles), out_shape...  7.44 us
  transfers between devices with their start and end apart: 7, of which 4 were waited for; matrix products, arithmetic and copies ran while one was open for 0% of the time, Pallas kernels for 11%

profile of v1, /device:TPU:8, one launch (start us, length us, event | category | flops | bytes accessed | tf_op | source)
XLA Modules:
  0.0 360.7 jit_solution(16891415619783774041)
XLA Ops:
  0.0 20.6 %pack.3.refs_0_ = bf16[32,20,16,128]{3,2,1,0:T(8,128)(2,1)} custom-call(bf16[8,80,8,512]{3,2,1,0:T(8,128)(2,1)} %x_ref.3), custom_call_target="tpu_custom_call" | custom-call | flops 52428800 | bytes 5242880 | tf_op jit(solution)/shard_map/pack/pallas_call | solution.py:58
  20.6 0.0 copy-start.7
  20.6 0.0 copy-start.8
  20.6 0.0 copy-start.9
  20.6 0.0 copy-start.10
  20.6 0.0 copy-start
  20.6 20.8 %pack.2.refs_1_ = bf16[32,20,16,128]{3,2,1,0:T(8,128)(2,1)} custom-call(bf16[8,80,8,512]{3,2,1,0:T(8,128)(2,1)} %x_ref.3), custom_call_target="tpu_custom_call" | custom-call | flops 52428800 | bytes 5242880 | tf_op jit(solution)/shard_map/pack/pallas_call | solution.py:58
  42.1 0.0 copy-done.7
  42.1 0.0 copy-done.8
  42.1 0.0 copy-done.9
  42.1 0.0 copy-done.10
  42.2 46.3 %all-gather.1.info_ref = f32[32,4,256]{2,1,0:T(4,128)S(1)} all-gather(f32[1,4,256]{2,1,0:T(4,128)S(1)} %maximum_bitcast_fusion), channel_id=2, replica_groups=mesh['member'=32,'tile'=8] {'member'}, dimensions={0}, use_global_device_ids=true | all-gather | bytes 135168 | tf_op jit(solution)/shard_map/all_gather | solution.py:327
  88.5 0.0 copy-done
  88.5 7.4 %gather_obs.1 = bf16[32,24,256]{2,1,0:T(8,128)(2,1)S(1)} custom-call(f32[32,4,256]{2,1,0:T(4,128)S(1)} %all-gather.1.info_ref, bf16[32,20,16,128]{3,2,1,0:T(8,128)(2,1)S(1)} %copy-done, bf16[32,20,16,128]{3,2,1,0:T(8,128)(2,1)} %pack.2.refs_1_), custom_call_target="tpu_custom_call" | custom-call | flops 1342177280 | bytes 6291456 | tf_op jit(solution)/shard_map/gather_obs/pallas_call | solution.py:150
  96.0 18.6 %all_to_all.25.own = bf16[32,24,256]{2,1,0:T(8,128)(2,1)S(1)} all-to-all(bf16[32,24,256]{2,1,0:T(8,128)(2,1)S(1)} %gather_obs.1), channel_id=1, replica_groups=mesh['member'=32,'tile'=8] {'member'}, dimensions={0} | all-to-all | bytes 786432 | tf_op jit(solution)/shard_map/all_to_all | solution.py:307
  114.6 56.2 %all_to_all.26.x_ref = bf16[32,20,16,128]{3,2,1,0:T(8,128)(2,1)} all-to-all(bf16[32,20,16,128]{3,2,1,0:T(8,128)(2,1)S(1)} %copy-done), channel_id=1, replica_groups=mesh['member'=32,'tile'=8] {'member'}, dimensions={0} | all-to-all | bytes 5242880 | tf_op jit(solution)/shard_map/all_to_all | solution.py:307
  170.8 5.1 %all-to-all-start = ((bf16[32,20,16,128]{3,2,1,0:T(8,128)(2,1)}), bf16[32,20,16,128]{3,2,1,0:T(8,128)(2,1)S(1)}, u32[]{:S(2)}, u32[]{:S(2)}) async-start(bf16[32,20,16,128]{3,2,1,0:T(8,128)(2,1)} %pack.2.refs_1_), calls=%async_computation | async-start | bytes 5242880 | tf_op jit(solution)/shard_map/all_to_all | solution.py:307
  175.9 1.9 collective-permute-start.1
  177.8 2.4 collective-permute-start
  180.3 0.0 copy-start.1
  180.3 3.4 collective-permute-start.3
  183.7 1.9 collective-permute-start.2
  185.7 0.0 collective-permute-done.3.above_info
  185.7 3.1 collective-permute-done.2.below_info
  188.7 0.0 collective-permute-done.1.above
  188.7 0.0 copy-start.4
  188.7 0.7 copy-done.4
  189.5 0.0 collective-permute-done.below
  189.5 0.0 copy-start.5
  189.5 1.0 copy-done.5
  190.5 10.9 %tile_weights.1 = (bf16[2,256,256]{2,1,0:T(8,128)(2,1)S(1)}, f32[2,256,128]{2,1,0:T(8,128)S(1)}) custom-call(bf16[32,24,256]{2,1,0:T(8,128)(2,1)S(1)} %all_to_all.25.own, bf16[32,24,256]{2,1,0:T(8,128)(2,1)} %collective-permute-done.below, bf16[32,24,256]{2,1,0:T(8,128)(2,1)S(1)} %copy-done.5, f32[3,4,256]{2,1,0:T(4,128)S(1)} %pad_maximum_fusion.own_info, ...), custom_call_target="tpu_custom_call" | custom-call | flops 5368709120 | bytes 3145728 | tf_op jit(solution)/shard_map/tile_weights/pallas_call | solution.py:252
  201.4 0.0 copy-done.1
  201.4 3.4 transform.3
  204.8 0.0 copy-start.2
  204.8 1.5 copy-done.2
  206.3 20.4 %all-to-all-done.x_ref = bf16[32,20,16,128]{3,2,1,0:T(8,128)(2,1)S(1)} async-done(((bf16[32,20,16,128]{3,2,1,0:T(8,128)(2,1)}), bf16[32,20,16,128]{3,2,1,0:T(8,128)(2,1)S(1)}, u32[]{:S(2)}, u32[]{:S(2)}) %all-to-all-start) | async-done | bytes 2621472 | tf_op jit(solution)/shard_map/all_to_all | solution.py:307
  226.7 6.1 %all-to-all-start.4 = ((bf16[32,20,16,128]{3,2,1,0:T(8,128)(2,1)}), bf16[32,20,16,128]{3,2,1,0:T(8,128)(2,1)}, u32[]{:S(2)}, u32[]{:S(2)}) async-start(bf16[32,20,16,128]{3,2,1,0:T(8,128)(2,1)} %copy-done.2), calls=%async_computation.4 | async-start | bytes 5242880 | tf_op jit(solution)/shard_map/all_to_all | solution.py:307
  232.8 3.4 transform.2
  236.2 0.0 copy-start.3
  236.2 1.5 copy-done.3
  237.8 46.4 %all-to-all-done.4.x_ref = bf16[32,20,16,128]{3,2,1,0:T(8,128)(2,1)} async-done(((bf16[32,20,16,128]{3,2,1,0:T(8,128)(2,1)}), bf16[32,20,16,128]{3,2,1,0:T(8,128)(2,1)}, u32[]{:S(2)}, u32[]{:S(2)}) %all-to-all-start.4) | async-done | bytes 2621472 | tf_op jit(solution)/shard_map/all_to_all | solution.py:307
  284.2 5.5 %all-to-all-start.2 = ((bf16[32,20,16,128]{3,2,1,0:T(8,128)(2,1)}), bf16[32,20,16,128]{3,2,1,0:T(8,128)(2,1)S(1)}, u32[]{:S(2)}, u32[]{:S(2)}) async-start(bf16[32,20,16,128]{3,2,1,0:T(8,128)(2,1)} %copy-done.3), calls=%async_computation.2 | async-start | bytes 5242880 | tf_op jit(solution)/shard_map/all_to_all | solution.py:307
  289.7 20.8 %unpack.2.rest_0_ = bf16[8,80,8,512]{3,2,1,0:T(8,128)(2,1)} custom-call(bf16[32,20,16,128]{3,2,1,0:T(8,128)(2,1)} %all-to-all-done.4.x_ref), custom_call_target="tpu_custom_call" | custom-call | flops 52428800 | bytes 5242880 | tf_op jit(solution)/shard_map/unpack/pallas_call | solution.py:101
  310.5 27.8 %all-to-all-done.2.x_ref = bf16[32,20,16,128]{3,2,1,0:T(8,128)(2,1)S(1)} async-done(((bf16[32,20,16,128]{3,2,1,0:T(8,128)(2,1)}), bf16[32,20,16,128]{3,2,1,0:T(8,128)(2,1)S(1)}, u32[]{:S(2)}, u32[]{:S(2)}) %all-to-all-start.2) | async-done | bytes 2621472 | tf_op jit(solution)/shard_map/all_to_all | solution.py:307
  338.3 0.0 copy-start.6
  338.3 1.5 copy-done.6
  339.8 20.9 %unpack.3 = bf16[8,80,8,512]{3,2,1,0:T(8,128)(2,1)} custom-call(bf16[32,20,16,128]{3,2,1,0:T(8,128)(2,1)} %copy-done.6, bf16[8,80,8,512]{3,2,1,0:T(8,128)(2,1)} %unpack.2.rest_0_), custom_call_target="tpu_custom_call", output_to_operand_aliasing={{}: (1, {})} | custom-call | flops 52428800 | bytes 5242880 | tf_op jit(solution)/shard_map/unpack/pallas_call | solution.py:101
  (5 shorter events, 0.0 us)
Async XLA Ops:
  20.6 21.5 %copy-start.7 = (f32[1,1,256]{2,1,0:T(1,128)S(1)}, f32[1,1,256]{2,1,0:T(1,128)}, u32[]{:S(2)}) copy-start(f32[1,1,256]{2,1,0:T(1,128)} %param.11) | copy-start | bytes 3076
  20.6 21.5 %copy-start.8 = (s32[1,1,256]{2,1,0:T(1,128)S(1)}, s32[1,1,256]{2,1,0:T(1,128)}, u32[]{:S(2)}) copy-start(s32[1,1,256]{2,1,0:T(1,128)} %param.8) | copy-start | bytes 3076
  20.6 21.5 %copy-start.9 = (s32[1,1,256]{2,1,0:T(1,128)S(1)}, s32[1,1,256]{2,1,0:T(1,128)}, u32[]{:S(2)}) copy-start(s32[1,1,256]{2,1,0:T(1,128)} %param.7) | copy-start | bytes 3076
  20.6 21.6 %copy-start.10 = (f32[1,1,256]{2,1,0:T(1,128)S(1)}, f32[1,1,256]{2,1,0:T(1,128)}, u32[]{:S(2)}) copy-start(f32[1,1,256]{2,1,0:T(1,128)} %param.10) | copy-start | bytes 3076
  20.6 67.9 %copy-start = (bf16[32,20,16,128]{3,2,1,0:T(8,128)(2,1)S(1)}, bf16[32,20,16,128]{3,2,1,0:T(8,128)(2,1)}, u32[]{:S(2)}) copy-start(bf16[32,20,16,128]{3,2,1,0:T(8,128)(2,1)} %pack.3.refs_0_) | copy-start | bytes 7864324
  170.8 55.9 %all-to-all-start = ((bf16[32,20,16,128]{3,2,1,0:T(8,128)(2,1)}), bf16[32,20,16,128]{3,2,1,0:T(8,128)(2,1)S(1)}, u32[]{:S(2)}, u32[]{:S(2)}) async-start(bf16[32,20,16,128]{3,2,1,0:T(8,128)(2,1)} %pack.2.refs_1_), calls=%async_computation | async-start | bytes 5242880 | tf_op jit(solution)/shard_map/all_to_all | solution.py:307
  175.9 12.9 %collective-permute-start.1 = (bf16[32,24,256]{2,1,0:T(8,128)(2,1)S(1)}, bf16[32,24,256]{2,1,0:T(8,128)(2,1)S(1)}, u32[]{:S(2)}, u32[]{:S(2)}) collective-permute-start(bf16[32,24,256]{2,1,0:T(8,128)(2,1)S(1)} %all_to_all.25.own), channel_id=1, source_target_pairs={{1,0},{2,1},{3,2},{4,3},{5,4},{6,5},{7,6},{9,8},{10,9},{11,10},{12... | collective-permute-start | bytes 1179656 | tf_op jit(solution)/shard_map/ppermute | solution.py:339
  177.8 11.7 %collective-permute-start = (bf16[32,24,256]{2,1,0:T(8,128)(2,1)S(1)}, bf16[32,24,256]{2,1,0:T(8,128)(2,1)}, u32[]{:S(2)}, u32[]{:S(2)}) collective-permute-start(bf16[32,24,256]{2,1,0:T(8,128)(2,1)S(1)} %all_to_all.25.own), channel_id=1, source_target_pairs={{0,1},{1,2},{2,3},{3,4},{4,5},{5,6},{6,7},{8,9},{9,10},{10,11},{11... | collective-permute-start | bytes 1179656 | tf_op jit(solution)/shard_map/ppermute | solution.py:339
  180.3 21.1 %copy-start.1 = (bf16[32,20,16,128]{3,2,1,0:T(8,128)(2,1)S(1)}, bf16[32,20,16,128]{3,2,1,0:T(8,128)(2,1)}, u32[]{:S(2)}) copy-start(bf16[32,20,16,128]{3,2,1,0:T(8,128)(2,1)} %all_to_all.26.x_ref) | copy-start | bytes 7864324
  180.3 5.4 %collective-permute-start.3 = (f32[3,4,256]{2,1,0:T(4,128)S(1)}, f32[3,4,256]{2,1,0:T(4,128)S(1)}, u32[]{:S(2)}, u32[]{:S(2)}) collective-permute-start(f32[3,4,256]{2,1,0:T(4,128)S(1)} %pad_maximum_fusion.own_info), channel_id=1, source_target_pairs={{1,0},{2,1},{3,2},{4,3},{5,4},{6,5},{7,6},{9,8},{10,9},{11,10},{12... | collective-permute-start | bytes 36872 | tf_op jit(solution)/shard_map/ppermute | solution.py:340
  183.7 5.0 %collective-permute-start.2 = (f32[3,4,256]{2,1,0:T(4,128)S(1)}, f32[3,4,256]{2,1,0:T(4,128)S(1)}, u32[]{:S(2)}, u32[]{:S(2)}) collective-permute-start(f32[3,4,256]{2,1,0:T(4,128)S(1)} %pad_maximum_fusion.own_info), channel_id=1, source_target_pairs={{0,1},{1,2},{2,3},{3,4},{4,5},{5,6},{6,7},{8,9},{9,10},{10,11},{11... | collective-permute-start | bytes 36872 | tf_op jit(solution)/shard_map/ppermute | solution.py:340
  188.7 0.7 copy-start.4
  189.5 1.0 copy-start.5
  204.8 1.5 copy-start.2
  226.7 57.5 %all-to-all-start.4 = ((bf16[32,20,16,128]{3,2,1,0:T(8,128)(2,1)}), bf16[32,20,16,128]{3,2,1,0:T(8,128)(2,1)}, u32[]{:S(2)}, u32[]{:S(2)}) async-start(bf16[32,20,16,128]{3,2,1,0:T(8,128)(2,1)} %copy-done.2), calls=%async_computation.4 | async-start | bytes 5242880 | tf_op jit(solution)/shard_map/all_to_all | solution.py:307
  236.2 1.5 copy-start.3
  284.2 54.1 %all-to-all-start.2 = ((bf16[32,20,16,128]{3,2,1,0:T(8,128)(2,1)}), bf16[32,20,16,128]{3,2,1,0:T(8,128)(2,1)S(1)}, u32[]{:S(2)}, u32[]{:S(2)}) async-start(bf16[32,20,16,128]{3,2,1,0:T(8,128)(2,1)} %copy-done.3), calls=%async_computation.2 | async-start | bytes 5242880 | tf_op jit(solution)/shard_map/all_to_all | solution.py:307
  338.3 1.5 copy-start.6

commit v2 on v1

--- a/solution.py
+++ b/solution.py
@@ -14,13 +14,15 @@
 LOC = 8
 MEM_DEV = 8
 LANES = 128
-CHUNKS = (20, 20)
+CHUNKS = (16, 12, 12)
+CARRIER = 1
+PER_STEP = 4
 NT = (((1,), (1,)), ((), ()))
 NN = (((1,), (0,)), ((), ()))
 VMEM_LIMIT = 48 * 1024 * 1024
 
 
-def swap_groups(parts, sign):
+def swap_groups(parts):
     lane_group = lax.broadcasted_iota(jnp.int32, parts[0].shape, 1) // LON_DEV
     parts = list(parts)
     for step in (4, 2, 1):
@@ -29,69 +31,88 @@
             if i & step:
                 continue
             a, b = parts[i], parts[i + step]
-            parts[i] = jnp.where(low, a, pltpu.roll(b, step * LON_DEV, 1))
-            parts[i + step] = jnp.where(low, pltpu.roll(a, LANES - step * LON_DEV, 1), b)
+            if step == 4:
+                crossed = pltpu.roll(jnp.where(low, b, a), 64, 1)
+                parts[i] = jnp.where(low, a, crossed)
+                parts[i + step] = jnp.where(low, crossed, b)
+            else:
+                parts[i] = jnp.where(low, a, pltpu.roll(b, step * LON_DEV, 1))
+                parts[i + step] = jnp.where(low, pltpu.roll(a, LANES - step * LON_DEV, 1), b)
     return parts
 
 
-def pack_kernel(per_step, x_ref, o_ref):
-    def pair(b, carry):
-        rows = []
+def lanes_of(g):
+    return pl.ds(pl.multiple_of(g * LANES, LANES), LANES)
+
+
+def pack_kernel(per_step, x_ref, o_ref, held):
+    def unit(t, carry):
+        b, g = t // 4, t % 4
         for e in range(2):
-            cells = x_ref[:, b * 2 + e].astype(jnp.float32)
-            rows.append(jnp.transpose(cells, (1, 0, 2)))
-        halves = []
-        for p in range(2):
-            halves.append(
-                swap_groups([rows[e][p * 4 + r] for e in range(2) for r in range(4)], 1)
-            )
-        for a in range(8):
-            both = jnp.concatenate([halves[0][a], halves[1][a]], axis=0)
-            o_ref[a, b] = both.astype(jnp.bfloat16)
+            cells = x_ref[:, b * 2 + e, :, lanes_of(g)].astype(jnp.float32)
+            held[t * 2 + e] = cells.reshape(64, LANES)
+        parts = []
+        for e in range(2):
+            for r in range(PATCH_LAT):
+                halves = [
+                    held[t * 2 + e, pl.ds(p * PATCH_LAT + r, MEM_DEV, stride=8), :]
+                    for p in range(2)
+                ]
+                parts.append(jnp.concatenate(halves, axis=0).astype(jnp.bfloat16))
+        for a, part in enumerate(swap_groups(parts)):
+            o_ref[g * 8 + a, b] = part
         return carry
 
-    lax.fori_loop(0, per_step, pair, 0)
-
-
-def pack(background, first, count, per_step):
-    base = first // per_step
+    lax.fori_loop(0, per_step * 4, unit, 0, unroll=8)
+
+
+def relayout_cost(count):
+    return pl.CostEstimate(
+        flops=count * 65536 * 40, bytes_accessed=count * 262144, transcendentals=0
+    )
+
+
+def pack(background, first, count, extra):
+    base = first // PER_STEP
     return pl.pallas_call(
-        functools.partial(pack_kernel, per_step),
-        out_shape=jax.ShapeDtypeStruct((32, count, 16, LANES), jnp.bfloat16),
-        grid=(count // per_step, 4),
+        functools.partial(pack_kernel, PER_STEP),
+        out_shape=jax.ShapeDtypeStruct((32, count + extra, 16, LANES), jnp.bfloat16),
+        grid=(count // PER_STEP,),
         in_specs=[
-            pl.BlockSpec((MEM_DEV, 2 * per_step, 8, LANES), lambda i, g: (0, base + i, 0, g))
+            pl.BlockSpec((MEM_DEV, 2 * PER_STEP, 8, 512), lambda i: (0, base + i, 0, 0))
         ],
-        out_specs=pl.BlockSpec((8, per_step, 16, LANES), lambda i, g: (g, i, 0, 0)),
-        cost_estimate=pl.CostEstimate(
-            flops=count * 65536 * 40, bytes_accessed=count * 262144, transcendentals=0
-        ),
+        out_specs=pl.BlockSpec((32, PER_STEP, 16, LANES), lambda i: (0, i, 0, 0)),
+        scratch_shapes=[pltpu.VMEM((8 * PER_STEP, 64, LANES), jnp.float32)],
+        compiler_params=pltpu.CompilerParams(vmem_limit_bytes=VMEM_LIMIT),
+        cost_estimate=relayout_cost(count),
         name="pack",
     )(background)
 
 
 def unpack_kernel(per_step, x_ref, *rest):
-    o_ref = rest[-1]
-
-    def pair(b, carry):
-        both = [x_ref[a, b].astype(jnp.float32) for a in range(8)]
-        rows = [[None] * 8, [None] * 8]
-        for p in range(2):
-            parts = swap_groups([both[a][p * 8 : (p + 1) * 8] for a in range(8)], -1)
-            for e in range(2):
-                for r in range(4):
-                    rows[e][p * 4 + r] = parts[e * 4 + r]
+    o_ref, held = rest[-2:]
+
+    def unit(t, carry):
+        b, g = t // 4, t % 4
+        parts = swap_groups([x_ref[g * 8 + a, b] for a in range(8)])
         for e in range(2):
-            cells = jnp.transpose(jnp.stack(rows[e], axis=0), (1, 0, 2))
-            o_ref[:, b * 2 + e] = cells.astype(jnp.bfloat16)
+            for r in range(PATCH_LAT):
+                both = parts[e * PATCH_LAT + r].astype(jnp.float32)
+                for p in range(2):
+                    held[t * 2 + e, pl.ds(p * PATCH_LAT + r, MEM_DEV, stride=8), :] = both[
+                        p * 8 : (p + 1) * 8
+                    ]
+        for e in range(2):
+            cells = held[t * 2 + e].reshape(MEM_DEV, 8, LANES)
+            o_ref[:, b * 2 + e, :, lanes_of(g)] = cells.astype(jnp.bfloat16)
         return carry
 
-    lax.fori_loop(0, per_step, pair, 0)
-
-
-def unpack(blocks, previous, first, count, per_step, shape):
-    base = first // per_step
-    in_specs = [pl.BlockSpec((8, per_step, 16, LANES), lambda i, g: (g, i, 0, 0))]
+    lax.fori_loop(0, per_step * 4, unit, 0, unroll=8)
+
+
+def unpack(blocks, previous, first, count, shape):
+    base = first // PER_STEP
+    in_specs = [pl.BlockSpec((32, PER_STEP, 16, LANES), lambda i: (0, i, 0, 0))]
     operands = [blocks]
     aliases = {}
     if previous is not None:
@@ -99,17 +120,17 @@
         operands.append(previous)
         aliases = {1: 0}
     return pl.pallas_call(
-        functools.partial(unpack_kernel, per_step),
+        functools.partial(unpack_kernel, PER_STEP),
         out_shape=jax.ShapeDtypeStruct(shape, jnp.bfloat16),
-        grid=(count // per_step, 4),
+        grid=(count // PER_STEP,),
         in_specs=in_specs,
         out_specs=pl.BlockSpec(
-            (MEM_DEV, 2 * per_step, 8, LANES), lambda i, g: (0, base + i, 0, g)
-        ),
+            (MEM_DEV, 2 * PER_STEP, 8, 512), lambda i: (0, base + i, 0, 0)
+        ),
+        scratch_shapes=[pltpu.VMEM((8 * PER_STEP, 64, LANES), jnp.float32)],
         input_output_aliases=aliases,
-        cost_estimate=pl.CostEstimate(
-            flops=count * 65536 * 40, bytes_accessed=count * 262144, transcendentals=0
-        ),
+        compiler_params=pltpu.CompilerParams(vmem_limit_bytes=VMEM_LIMIT),
+        cost_estimate=relayout_cost(count),
         name="unpack",
     )(*operands)
 
@@ -129,15 +150,18 @@
         total = jnp.zeros((MEM_DEV, 256), jnp.float32)
         first = 0
         for block, count in zip(blocks, counts):
-            rows = block[t].reshape(count * 16, LANES)
+            rows = block[t, :count].reshape(count * 16, LANES)
             found = lax.dot_general(rows, pick, NN, preferred_element_type=jnp.float32)
             found = found.reshape(count * 2, MEM_DEV, 256)
             for g in range(count * 2):
                 total = total + jnp.where(group == first * 2 + g, found[g], 0.0)
             first += count
-        held[lax.rem(a + 1, 32), 0:8] = total
-        held[a, 8:16] = total
-        held[lax.rem(a + 31, 32), 16:24] = total
+        for half in range(2):
+            part = total[:, half * LANES : (half + 1) * LANES]
+            rows = pl.ds(half * 8, 8)
+            held[lax.rem(a + 1, 32), 0, rows] = part
+            held[a, 1, rows] = part
+            held[lax.rem(a + 31, 32), 2, rows] = part
 
     @pl.when(step == 32 // tiles - 1)
     def _():
@@ -145,16 +169,18 @@
 
 
 def gather_obs(info, blocks):
-    counts = tuple(b.shape[1] for b in blocks)
     tiles = 4
+    carrier = blocks[CARRIER]
+    place = CHUNKS[CARRIER] // 3
     return pl.pallas_call(
-        functools.partial(gather_kernel, counts, tiles),
-        out_shape=jax.ShapeDtypeStruct((32, 24, 256), jnp.bfloat16),
+        functools.partial(gather_kernel, CHUNKS, tiles),
+        out_shape=jax.ShapeDtypeStruct(carrier.shape, jnp.bfloat16),
         grid=(32 // tiles,),
         in_specs=[pl.BlockSpec((32, 4, 256), lambda i: (0, 0, 0))]
-        + [pl.BlockSpec((tiles, c, 16, LANES), lambda i: (i, 0, 0, 0)) for c in counts],
-        out_specs=pl.BlockSpec((32, 24, 256), lambda i: (0, 0, 0)),
-        scratch_shapes=[pltpu.VMEM((32, 24, 256), jnp.float32)],
+        + [pl.BlockSpec((tiles,) + b.shape[1:], lambda i: (i, 0, 0, 0)) for b in blocks],
+        out_specs=pl.BlockSpec((32, 3, 16, LANES), lambda i: (0, place, 0, 0)),
+        scratch_shapes=[pltpu.VMEM((32, 3, 16, LANES), jnp.float32)],
+        input_output_aliases={1 + CARRIER: 0},
         compiler_params=pltpu.CompilerParams(vmem_limit_bytes=VMEM_LIMIT),
         cost_estimate=pl.CostEstimate(
             flops=2 * 32 * 640 * 256 * 128, bytes_accessed=6 << 20, transcendentals=0
@@ -191,8 +217,10 @@
         lat_shift = (j - 1.0) * LAT_DEV
         for i in range(3):
             lon_shift = (i - 1.0) * LON_DEV
-            hx = values[...].astype(jnp.float32).reshape(32, 3, MEM_DEV, 256)[:, i]
-            hx = hx.reshape(members, 256)
+            halves = values[:, i].astype(jnp.float32).reshape(32, 2, MEM_DEV, LANES)
+            hx = jnp.concatenate(
+                [halves[:, half].reshape(members, LANES) for half in range(2)], axis=1
+            )
             centre = jnp.sum(hx, axis=0, keepdims=True) * (1.0 / members)
             y = hx - centre
             y_parts = split(y)
@@ -248,15 +276,24 @@
 
 
 def tile_weights(values, infos):
-    vmem = pl.BlockSpec(memory_space=pltpu.VMEM)
+    place = CHUNKS[CARRIER] // 3
     return pl.pallas_call(
         weights_kernel,
         out_shape=(
             jax.ShapeDtypeStruct((2, 256, 256), jnp.bfloat16),
             jax.ShapeDtypeStruct((2, 256, LANES), jnp.float32),
         ),
-        in_specs=[vmem] * 6,
-        out_specs=(vmem, vmem),
+        grid=(1,),
+        in_specs=[
+            pl.BlockSpec((32, 3, 16, LANES), lambda i: (0, place, 0, 0)),
+            pl.BlockSpec((32, 3, 16, LANES), lambda i: (0, 0, 0, 0)),
+            pl.BlockSpec((32, 3, 16, LANES), lambda i: (0, 0, 0, 0)),
+        ]
+        + [pl.BlockSpec((3, 4, 256), lambda i: (0, 0, 0))] * 3,
+        out_specs=(
+            pl.BlockSpec((2, 256, 256), lambda i: (0, 0, 0)),
+            pl.BlockSpec((2, 256, LANES), lambda i: (0, 0, 0)),
+        ),
         scratch_shapes=[pltpu.VMEM((2, 256, 256), jnp.float32)],
         compiler_params=pltpu.CompilerParams(vmem_limit_bytes=VMEM_LIMIT),
         cost_estimate=pl.CostEstimate(
@@ -282,12 +319,11 @@
         o_ref[:, b] = result.astype(jnp.bfloat16)
 
 
-def transform(blocks, weights, keep, per_step):
-    count = blocks.shape[1]
+def transform(blocks, count, weights, keep, per_step):
     spec = pl.BlockSpec((32, per_step, 16, LANES), lambda i: (0, i, 0, 0))
     return pl.pallas_call(
         functools.partial(transform_kernel, per_step),
-        out_shape=jax.ShapeDtypeStruct(blocks.shape, jnp.bfloat16),
+        out_shape=jax.ShapeDtypeStruct((32, count, 16, LANES), jnp.bfloat16),
         grid=(count // per_step,),
         in_specs=[
             spec,
@@ -311,8 +347,10 @@
     firsts = [sum(CHUNKS[:n]) for n in range(len(CHUNKS))]
     slots = obs_cell.shape[-1]
     members = 256
-    blocks = [pack(background, f, c, 5) for f, c in zip(firsts, CHUNKS)]
-    arrived = [exchange(b) for b in blocks]
+    blocks = [
+        pack(background, f, c, 3 if n == CARRIER else 0)
+        for n, (f, c) in enumerate(zip(firsts, CHUNKS))
+    ]
 
     inside = (jnp.arange(slots, dtype=jnp.int32) < obs_count[0, 0]).astype(jnp.float32)
     weight = inside * obs_precision[0, 0] / (members - 1.0)
@@ -324,8 +362,10 @@
             weight,
         ]
     )
-    info = lax.all_gather(own, "member")
-    hx = exchange(gather_obs(info, blocks))
+    info = exchange(jnp.broadcast_to(own[None], (32,) + own.shape))
+    blocks[CARRIER] = gather_obs(info, blocks)
+    arrived = [exchange(b) for b in blocks]
+    hx = arrived[CARRIER][:, CHUNKS[CARRIER] :]
     me = lax.axis_index("member")
     near = jnp.stack(
         [
@@ -336,14 +376,16 @@
     bands = lax.axis_size("tile")
     up = [(i, i + 1) for i in range(bands - 1)]
     down = [(i + 1, i) for i in range(bands - 1)]
-    values = (hx, lax.ppermute(hx, "tile", up), lax.ppermute(hx, "tile", down))
+    values = (arrived[CARRIER], lax.ppermute(hx, "tile", up), lax.ppermute(hx, "tile", down))
     infos = (near, lax.ppermute(near, "tile", up), lax.ppermute(near, "tile", down))
     weights, keep = tile_weights(values, infos)
 
-    back = [exchange(transform(b, weights, keep, 2)) for b in arrived]
+    back = [
+        exchange(transform(b, c, weights, keep, 4)) for b, c in zip(arrived, CHUNKS)
+    ]
     out = None
     for b, f, c in zip(back, firsts, CHUNKS):
-        out = unpack(b, out, f, c, 5, background.shape)
+        out = unpack(b, out, f, c, background.shape)
     return out
 
 

time: 363 us -> 319 us (0.88)
  blocking collectives: 121 us -> 52.4 us
  waiting for transfers between devices: 97.7 us -> 156 us
  Pallas kernels: 108 us -> 52.1 us
  starting transfers between devices: 26.4 us -> 47.9 us
    all_to_all x3 -> x6, waiting for transfers between devices: 94.6 us -> 153 us  [exchange(): lax.all_to_all(blocks, 'member', split_axis=0, concat_axis=0, tiled=True)]
    pallas_call x5 -> x7, Pallas kernels: 90.5 us -> 34.3 us  [the longest x3 13.8 us: pack(): pl.pallas_call(functools.partial(pack_kernel, PER_STEP), out_shape=jax.Sh...]
    all_gather x1 -> x0, blocking collectives: 46.3 us -> none  [per_device(): info = lax.all_gather(own, 'member')]
    all_to_all x2 -> x1, blocking collectives: 74.9 us -> 52.4 us  [exchange(): lax.all_to_all(blocks, 'member', split_axis=0, concat_axis=0, tiled=True)]
    all_to_all x3 -> x6, starting transfers between devices: 16.7 us -> 38.3 us  [exchange(): lax.all_to_all(blocks, 'member', split_axis=0, concat_axis=0, tiled=True)]
    pallas_call x2 -> x3, Pallas kernels: 6.75 us -> 7.94 us  [transform(): pl.pallas_call(functools.partial(transform_kernel, per_step), out_shape=j...]
  transfers between devices with their start and end apart: 7 -> 10, of which waited for: 4 -> 7; matrix products, arithmetic and copies ran while one was open for 0% -> 0% of each run, Pallas kernels for 11% -> 15%
where the time goes in v2:
time: 319 us; the launch traced here: 318 us
  waiting for transfers between devices  156 us (49%)
  blocking collectives  52.4 us (16%)
  Pallas kernels  52.1 us (16%)
  starting transfers between devices  47.9 us (15%)
  local copies, waits for them, and re-layouts  7.16 us (2%)
    all_to_all x6, waiting for transfers between devices, exchange(): lax.all_to_all(blocks, 'member', split_axis=0, concat_axis=0, tiled=True)  153 us
    all_to_all x1, blocking collectives, exchange(): lax.all_to_all(blocks, 'member', split_axis=0, concat_axis=0, tiled=True)  52.4 us
    all_to_all x6, starting transfers between devices, exchange(): lax.all_to_all(blocks, 'member', split_axis=0, concat_axis=0, tiled=True)  38.3 us
    pallas_call x3, Pallas kernels, pack(): pl.pallas_call(functools.partial(pack_kernel, PER_STEP), out_shape=jax.Sh...  13.8 us
    pallas_call x3, Pallas kernels, unpack(): pl.pallas_call(functools.partial(unpack_kernel, PER_STEP), out_shape=jax....  12.6 us
    pallas_call x1, Pallas kernels, tile_weights(): pl.pallas_call(weights_kernel, out_shape=(jax.ShapeDtypeStruct((2, 256, 2...  9.9 us
    pallas_call x3, Pallas kernels, transform(): pl.pallas_call(functools.partial(transform_kernel, per_step), out_shape=j...  7.94 us
    pallas_call x1, Pallas kernels, gather_obs(): pl.pallas_call(functools.partial(gather_kernel, CHUNKS, tiles), out_shape...  7.83 us
  transfers between devices with their start and end apart: 10, of which 7 were waited for; matrix products, arithmetic and copies ran while one was open for 0% of the time, Pallas kernels for 15%

profile of v2, /device:TPU:8, one launch (start us, length us, event | category | flops | bytes accessed | tf_op | source)
XLA Modules:
  0.0 318.1 jit_solution(12301545922924765559)
XLA Ops:
  0.7 0.7 fusion
  1.3 0.7 convert_bitcast_fusion
  2.0 0.7 pad_maximum_fusion.1
  2.7 0.7 broadcast_in_dim.2
  3.4 11.3 %all-to-all-start.1 = ((f32[32,4,256]{2,1,0:T(4,128)}), f32[32,4,256]{2,1,0:T(4,128)S(1)}, u32[]{:S(2)}, u32[]{:S(2)}) async-start(f32[32,4,256]{2,1,0:T(4,128)} %broadcast_in_dim.2), calls=%async_computation.1 | async-start | bytes 262144 | tf_op jit(solution)/shard_map/all_to_all | solution.py:343
  14.7 4.6 %pack.3.refs_2_ = bf16[32,12,16,128]{3,2,1,0:T(8,128)(2,1)} custom-call(bf16[8,80,8,512]{3,2,1,0:T(8,128)(2,1)} %x_ref.5), custom_call_target="tpu_custom_call" | custom-call | flops 31457280 | bytes 3145728 | tf_op jit(solution)/shard_map/pack/pallas_call | solution.py:77
  19.3 5.9 %all-to-all-done.1.info_ref = f32[32,4,256]{2,1,0:T(4,128)S(1)} async-done(((f32[32,4,256]{2,1,0:T(4,128)}), f32[32,4,256]{2,1,0:T(4,128)S(1)}, u32[]{:S(2)}, u32[]{:S(2)}) %all-to-all-start.1) | async-done | bytes 131104 | tf_op jit(solution)/shard_map/all_to_all | solution.py:343
  25.2 0.0 copy-start.7
  25.2 0.7 copy-done.7
  25.8 4.0 %all-to-all-start = ((bf16[32,12,16,128]{3,2,1,0:T(8,128)(2,1)}), bf16[32,12,16,128]{3,2,1,0:T(8,128)(2,1)S(1)}, u32[]{:S(2)}, u32[]{:S(2)}) async-start(bf16[32,12,16,128]{3,2,1,0:T(8,128)(2,1)} %pack.3.refs_2_), calls=%async_computation | async-start | bytes 3145728 | tf_op jit(solution)/shard_map/all_to_all | solution.py:343
  29.8 3.8 %pack.5.refs_1_ = bf16[32,15,16,128]{3,2,1,0:T(8,128)(2,1)S(1)} custom-call(bf16[8,80,8,512]{3,2,1,0:T(8,128)(2,1)} %x_ref.5), custom_call_target="tpu_custom_call" | custom-call | flops 31457280 | bytes 3145728 | tf_op jit(solution)/shard_map/pack/pallas_call | solution.py:77
  33.7 0.0 copy-start.8
  33.7 5.4 %pack.4.refs_0_ = bf16[32,16,16,128]{3,2,1,0:T(8,128)(2,1)} custom-call(bf16[8,80,8,512]{3,2,1,0:T(8,128)(2,1)} %x_ref.5), custom_call_target="tpu_custom_call" | custom-call | flops 41943040 | bytes 4194304 | tf_op jit(solution)/shard_map/pack/pallas_call | solution.py:77
  39.1 0.0 copy-done.8
  39.1 7.8 %gather_obs.1 = bf16[32,15,16,128]{3,2,1,0:T(8,128)(2,1)S(1)} custom-call(f32[32,4,256]{2,1,0:T(4,128)S(1)} %copy-done.8, bf16[32,16,16,128]{3,2,1,0:T(8,128)(2,1)} %pack.4.refs_0_, bf16[32,15,16,128]{3,2,1,0:T(8,128)(2,1)S(1)} %pack.5.refs_1_, bf16[32,12,16,128]{3,2,1,0:T(8,128)(2,1)} %pack.3.refs_2_), custom_call_target="tpu_custom_call", output_to_operand_aliasing={{}: (2, {})} | custom-call | flops 1342177280 | bytes 6291456 | tf_op jit(solution)/shard_map/gather_obs/pallas_call | solution.py:175
  46.9 21.4 %all-to-all-done.x_ref = bf16[32,12,16,128]{3,2,1,0:T(8,128)(2,1)S(1)} async-done(((bf16[32,12,16,128]{3,2,1,0:T(8,128)(2,1)}), bf16[32,12,16,128]{3,2,1,0:T(8,128)(2,1)S(1)}, u32[]{:S(2)}, u32[]{:S(2)}) %all-to-all-start) | async-done | bytes 1572896 | tf_op jit(solution)/shard_map/all_to_all | solution.py:343
  68.3 0.0 copy-start.2
  68.3 52.4 %all_to_all.35.own.x_ref = bf16[32,15,16,128]{3,2,1,0:T(8,128)(2,1)} all-to-all(bf16[32,15,16,128]{3,2,1,0:T(8,128)(2,1)S(1)} %gather_obs.1), channel_id=1, replica_groups=mesh['member'=32,'tile'=8] {'member'}, dimensions={0} | all-to-all | bytes 3932160 | tf_op jit(solution)/shard_map/all_to_all | solution.py:343
  120.7 0.0 copy-done.2
  120.7 0.0 copy-start
  120.7 5.3 %all-to-all-start.5 = ((bf16[32,16,16,128]{3,2,1,0:T(8,128)(2,1)}), bf16[32,16,16,128]{3,2,1,0:T(8,128)(2,1)}, u32[]{:S(2)}, u32[]{:S(2)}) async-start(bf16[32,16,16,128]{3,2,1,0:T(8,128)(2,1)} %pack.4.refs_0_), calls=%async_computation.5 | async-start | bytes 4194304 | tf_op jit(solution)/shard_map/all_to_all | solution.py:343
  126.0 0.0 copy-done
  126.1 1.9 collective-permute-start.1
  128.0 2.4 collective-permute-start
  130.4 0.7 constant_dynamic-slice_fusion.2
  131.2 3.2 collective-permute-start.3
  134.3 2.1 collective-permute-start.2
  136.5 0.0 collective-permute-done.3.above_info
  136.5 2.9 collective-permute-done.2.below_info
  139.4 0.0 collective-permute-done.1.above
  139.4 0.0 collective-permute-done.below
  139.4 9.9 %tile_weights.1 = (bf16[2,256,256]{2,1,0:T(8,128)(2,1)S(1)}, f32[2,256,128]{2,1,0:T(8,128)S(1)}) custom-call(bf16[32,15,16,128]{3,2,1,0:T(8,128)(2,1)S(1)} %copy-done, bf16[32,3,16,128]{3,2,1,0:T(8,128)(2,1)S(1)} %collective-permute-done.below, bf16[32,3,16,128]{3,2,1,0:T(8,128)(2,1)S(1)} %collective-permute-done.1.above, ...), custom_call_target="tpu_custom_call" | custom-call | flops 5368709120 | bytes 3145728 | tf_op jit(solution)/shard_map/tile_weights/pallas_call | solution.py:280
  149.3 2.8 transform.4
  152.1 22.2 %all-to-all-done.5.x_ref = bf16[32,16,16,128]{3,2,1,0:T(8,128)(2,1)} async-done(((bf16[32,16,16,128]{3,2,1,0:T(8,128)(2,1)}), bf16[32,16,16,128]{3,2,1,0:T(8,128)(2,1)}, u32[]{:S(2)}, u32[]{:S(2)}) %all-to-all-start.5) | async-done | bytes 2097184 | tf_op jit(solution)/shard_map/all_to_all | solution.py:343
  174.3 5.9 %all-to-all-start.4 = ((bf16[32,12,16,128]{3,2,1,0:T(8,128)(2,1)}), bf16[32,12,16,128]{3,2,1,0:T(8,128)(2,1)S(1)}, u32[]{:S(2)}, u32[]{:S(2)}) async-start(bf16[32,12,16,128]{3,2,1,0:T(8,128)(2,1)} %transform.4), calls=%async_computation.4 | async-start | bytes 3145728 | tf_op jit(solution)/shard_map/all_to_all | solution.py:343
  180.2 3.6 %transform.5 = bf16[32,16,16,128]{3,2,1,0:T(8,128)(2,1)S(1)} custom-call(bf16[32,16,16,128]{3,2,1,0:T(8,128)(2,1)} %all-to-all-done.5.x_ref, bf16[2,256,256]{2,1,0:T(8,128)(2,1)S(1)} %get-tuple-element.7.w_ref, f32[2,256,128]{2,1,0:T(8,128)S(1)} %get-tuple-element.8.keep_ref), custom_call_target="tpu_custom_call" | custom-call | flops 536870912 | bytes 4194304 | tf_op jit(solution)/shard_map/transform/pallas_call | solution.py:324
  183.8 0.0 copy-start.1
  183.8 1.3 copy-done.1
  185.1 31.5 %all-to-all-done.4.x_ref = bf16[32,12,16,128]{3,2,1,0:T(8,128)(2,1)S(1)} async-done(((bf16[32,12,16,128]{3,2,1,0:T(8,128)(2,1)}), bf16[32,12,16,128]{3,2,1,0:T(8,128)(2,1)S(1)}, u32[]{:S(2)}, u32[]{:S(2)}) %all-to-all-start.4) | async-done | bytes 1572896 | tf_op jit(solution)/shard_map/all_to_all | solution.py:343
  216.7 0.0 copy-start.5
  216.7 1.2 copy-done.5
  217.8 5.8 %all-to-all-start.6 = ((bf16[32,16,16,128]{3,2,1,0:T(8,128)(2,1)}), bf16[32,16,16,128]{3,2,1,0:T(8,128)(2,1)S(1)}, u32[]{:S(2)}, u32[]{:S(2)}) async-start(bf16[32,16,16,128]{3,2,1,0:T(8,128)(2,1)} %copy-done.1), calls=%async_computation.6 | async-start | bytes 4194304 | tf_op jit(solution)/shard_map/all_to_all | solution.py:343
  223.6 0.0 copy-start.3
  223.6 1.4 copy-done.3
  225.0 1.6 transform.3
  226.6 0.0 copy-start.4
  226.6 1.2 copy-done.4
  227.8 43.2 %all-to-all-done.6.x_ref = bf16[32,16,16,128]{3,2,1,0:T(8,128)(2,1)S(1)} async-done(((bf16[32,16,16,128]{3,2,1,0:T(8,128)(2,1)}), bf16[32,16,16,128]{3,2,1,0:T(8,128)(2,1)S(1)}, u32[]{:S(2)}, u32[]{:S(2)}) %all-to-all-start.6) | async-done | bytes 2097184 | tf_op jit(solution)/shard_map/all_to_all | solution.py:343
  271.0 6.1 %all-to-all-start.3 = ((bf16[32,12,16,128]{3,2,1,0:T(8,128)(2,1)}), bf16[32,12,16,128]{3,2,1,0:T(8,128)(2,1)}, u32[]{:S(2)}, u32[]{:S(2)}) async-start(bf16[32,12,16,128]{3,2,1,0:T(8,128)(2,1)} %copy-done.4), calls=%async_computation.3 | async-start | bytes 3145728 | tf_op jit(solution)/shard_map/all_to_all | solution.py:343
  277.0 0.0 copy-start.6
  277.1 4.4 %unpack.3.rest_0_ = bf16[8,80,8,512]{3,2,1,0:T(8,128)(2,1)} custom-call(bf16[32,16,16,128]{3,2,1,0:T(8,128)(2,1)S(1)} %all-to-all-done.6.x_ref), custom_call_target="tpu_custom_call" | custom-call | flops 41943040 | bytes 4194304 | tf_op jit(solution)/shard_map/unpack/pallas_call | solution.py:122
  281.4 0.0 copy-done.6
  281.5 3.5 %unpack.4.rest_0_ = bf16[8,80,8,512]{3,2,1,0:T(8,128)(2,1)} custom-call(bf16[32,12,16,128]{3,2,1,0:T(8,128)(2,1)S(1)} %copy-done.6, bf16[8,80,8,512]{3,2,1,0:T(8,128)(2,1)} %unpack.3.rest_0_), custom_call_target="tpu_custom_call", output_to_operand_aliasing={{}: (1, {})} | custom-call | flops 31457280 | bytes 3145728 | tf_op jit(solution)/shard_map/unpack/pallas_call | solution.py:122
  284.9 28.4 %all-to-all-done.3.x_ref = bf16[32,12,16,128]{3,2,1,0:T(8,128)(2,1)} async-done(((bf16[32,12,16,128]{3,2,1,0:T(8,128)(2,1)}), bf16[32,12,16,128]{3,2,1,0:T(8,128)(2,1)}, u32[]{:S(2)}, u32[]{:S(2)}) %all-to-all-start.3) | async-done | bytes 1572896 | tf_op jit(solution)/shard_map/all_to_all | solution.py:343
  313.3 4.7 %unpack.5 = bf16[8,80,8,512]{3,2,1,0:T(8,128)(2,1)} custom-call(bf16[32,12,16,128]{3,2,1,0:T(8,128)(2,1)} %all-to-all-done.3.x_ref, bf16[8,80,8,512]{3,2,1,0:T(8,128)(2,1)} %unpack.4.rest_0_), custom_call_target="tpu_custom_call", output_to_operand_aliasing={{}: (1, {})} | custom-call | flops 31457280 | bytes 3145728 | tf_op jit(solution)/shard_map/unpack/pallas_call | solution.py:122
  (2 shorter events, 0.0 us)
Async XLA Ops:
  3.4 21.8 %all-to-all-start.1 = ((f32[32,4,256]{2,1,0:T(4,128)}), f32[32,4,256]{2,1,0:T(4,128)S(1)}, u32[]{:S(2)}, u32[]{:S(2)}) async-start(f32[32,4,256]{2,1,0:T(4,128)} %broadcast_in_dim.2), calls=%async_computation.1 | async-start | bytes 262144 | tf_op jit(solution)/shard_map/all_to_all | solution.py:343
  25.2 0.7 copy-start.7
  25.8 42.5 %all-to-all-start = ((bf16[32,12,16,128]{3,2,1,0:T(8,128)(2,1)}), bf16[32,12,16,128]{3,2,1,0:T(8,128)(2,1)S(1)}, u32[]{:S(2)}, u32[]{:S(2)}) async-start(bf16[32,12,16,128]{3,2,1,0:T(8,128)(2,1)} %pack.3.refs_2_), calls=%async_computation | async-start | bytes 3145728 | tf_op jit(solution)/shard_map/all_to_all | solution.py:343
  33.7 5.4 %copy-start.8 = (f32[32,4,256]{2,1,0:T(4,128)S(1)}, f32[32,4,256]{2,1,0:T(4,128)}, u32[]{:S(2)}) copy-start(f32[32,4,256]{2,1,0:T(4,128)} %copy-done.7) | copy-start | bytes 393220
  68.3 52.4 %copy-start.2 = (bf16[32,12,16,128]{3,2,1,0:T(8,128)(2,1)}, bf16[32,12,16,128]{3,2,1,0:T(8,128)(2,1)S(1)}, u32[]{:S(2)}) copy-start(bf16[32,12,16,128]{3,2,1,0:T(8,128)(2,1)S(1)} %all-to-all-done.x_ref) | copy-start | bytes 4718596
  120.7 5.3 %copy-start = (bf16[32,15,16,128]{3,2,1,0:T(8,128)(2,1)S(1)}, bf16[32,15,16,128]{3,2,1,0:T(8,128)(2,1)}, u32[]{:S(2)}) copy-start(bf16[32,15,16,128]{3,2,1,0:T(8,128)(2,1)} %all_to_all.35.own.x_ref) | copy-start | bytes 5898244
  120.7 53.5 %all-to-all-start.5 = ((bf16[32,16,16,128]{3,2,1,0:T(8,128)(2,1)}), bf16[32,16,16,128]{3,2,1,0:T(8,128)(2,1)}, u32[]{:S(2)}, u32[]{:S(2)}) async-start(bf16[32,16,16,128]{3,2,1,0:T(8,128)(2,1)} %pack.4.refs_0_), calls=%async_computation.5 | async-start | bytes 4194304 | tf_op jit(solution)/shard_map/all_to_all | solution.py:343
  126.1 13.3 %collective-permute-start.1 = (bf16[32,3,16,128]{3,2,1,0:T(8,128)(2,1)S(1)}, bf16[32,3,16,128]{3,2,1,0:T(8,128)(2,1)S(1)}, u32[]{:S(2)}, u32[]{:S(2)}) collective-permute-start(bf16[32,3,16,128]{3,2,1,0:T(8,128)(2,1)S(1)} %slice.4), channel_id=1, source_target_pairs={{1,0},{2,1},{3,2},{4,3},{5,4},{6,5},{7,6},{9,8},{10,9},{11,10},{12... | collective-permute-start | bytes 1179656 | tf_op jit(solution)/shard_map/ppermute | solution.py:379
  128.0 11.4 %collective-permute-start = (bf16[32,3,16,128]{3,2,1,0:T(8,128)(2,1)S(1)}, bf16[32,3,16,128]{3,2,1,0:T(8,128)(2,1)S(1)}, u32[]{:S(2)}, u32[]{:S(2)}) collective-permute-start(bf16[32,3,16,128]{3,2,1,0:T(8,128)(2,1)S(1)} %slice.4), channel_id=1, source_target_pairs={{0,1},{1,2},{2,3},{3,4},{4,5},{5,6},{6,7},{8,9},{9,10},{10,11},{11... | collective-permute-start | bytes 1179656 | tf_op jit(solution)/shard_map/ppermute | solution.py:379
  131.2 5.3 %collective-permute-start.3 = (f32[3,4,256]{2,1,0:T(4,128)S(1)}, f32[3,4,256]{2,1,0:T(4,128)S(1)}, u32[]{:S(2)}, u32[]{:S(2)}) collective-permute-start(f32[3,4,256]{2,1,0:T(4,128)S(1)} %pad_maximum_fusion.own_info), channel_id=1, source_target_pairs={{1,0},{2,1},{3,2},{4,3},{5,4},{6,5},{7,6},{9,8},{10,9},{11,10},{12... | collective-permute-start | bytes 36872 | tf_op jit(solution)/shard_map/ppermute | solution.py:380
  134.3 5.0 %collective-permute-start.2 = (f32[3,4,256]{2,1,0:T(4,128)S(1)}, f32[3,4,256]{2,1,0:T(4,128)S(1)}, u32[]{:S(2)}, u32[]{:S(2)}) collective-permute-start(f32[3,4,256]{2,1,0:T(4,128)S(1)} %pad_maximum_fusion.own_info), channel_id=1, source_target_pairs={{0,1},{1,2},{2,3},{3,4},{4,5},{5,6},{6,7},{8,9},{9,10},{10,11},{11... | collective-permute-start | bytes 36872 | tf_op jit(solution)/shard_map/ppermute | solution.py:380
  174.3 42.4 %all-to-all-start.4 = ((bf16[32,12,16,128]{3,2,1,0:T(8,128)(2,1)}), bf16[32,12,16,128]{3,2,1,0:T(8,128)(2,1)S(1)}, u32[]{:S(2)}, u32[]{:S(2)}) async-start(bf16[32,12,16,128]{3,2,1,0:T(8,128)(2,1)} %transform.4), calls=%async_computation.4 | async-start | bytes 3145728 | tf_op jit(solution)/shard_map/all_to_all | solution.py:343
  183.8 1.3 copy-start.1
  216.7 1.2 copy-start.5
  217.8 53.1 %all-to-all-start.6 = ((bf16[32,16,16,128]{3,2,1,0:T(8,128)(2,1)}), bf16[32,16,16,128]{3,2,1,0:T(8,128)(2,1)S(1)}, u32[]{:S(2)}, u32[]{:S(2)}) async-start(bf16[32,16,16,128]{3,2,1,0:T(8,128)(2,1)} %copy-done.1), calls=%async_computation.6 | async-start | bytes 4194304 | tf_op jit(solution)/shard_map/all_to_all | solution.py:343
  223.6 1.4 copy-start.3
  226.6 1.2 copy-start.4
  271.0 42.4 %all-to-all-start.3 = ((bf16[32,12,16,128]{3,2,1,0:T(8,128)(2,1)}), bf16[32,12,16,128]{3,2,1,0:T(8,128)(2,1)}, u32[]{:S(2)}, u32[]{:S(2)}) async-start(bf16[32,12,16,128]{3,2,1,0:T(8,128)(2,1)} %copy-done.4), calls=%async_computation.3 | async-start | bytes 3145728 | tf_op jit(solution)/shard_map/all_to_all | solution.py:343
  277.0 4.4 %copy-start.6 = (bf16[32,12,16,128]{3,2,1,0:T(8,128)(2,1)S(1)}, bf16[32,12,16,128]{3,2,1,0:T(8,128)(2,1)}, u32[]{:S(2)}) copy-start(bf16[32,12,16,128]{3,2,1,0:T(8,128)(2,1)} %copy-done.5) | copy-start | bytes 4718596

commit v3 on v2

--- a/solution.py
+++ b/solution.py
@@ -14,7 +14,7 @@
 LOC = 8
 MEM_DEV = 8
 LANES = 128
-CHUNKS = (16, 12, 12)
+CHUNKS = (20, 12, 8)
 CARRIER = 1
 PER_STEP = 4
 NT = (((1,), (1,)), ((), ()))
@@ -45,7 +45,7 @@
     return pl.ds(pl.multiple_of(g * LANES, LANES), LANES)
 
 
-def pack_kernel(per_step, x_ref, o_ref, held):
+def pack_block(per_step, held, x_ref, o_ref):
     def unit(t, carry):
         b, g = t // 4, t % 4
         for e in range(2):
@@ -66,27 +66,52 @@
     lax.fori_loop(0, per_step * 4, unit, 0, unroll=8)
 
 
+def pack_kernel(turn, ranges, parity_ref, x_ref, *refs):
+    outs, held = refs[-1 - len(ranges) : -1], refs[-1]
+
+    @pl.when(parity_ref[0] == turn)
+    def _():
+        for (first, count), o_ref in zip(ranges, outs):
+            base = first // PER_STEP
+            pltpu.emit_pipeline(
+                functools.partial(pack_block, PER_STEP, held),
+                grid=(count // PER_STEP,),
+                in_specs=[
+                    pl.BlockSpec(
+                        (MEM_DEV, 2 * PER_STEP, 8, 512), lambda i, base=base: (0, base + i, 0, 0)
+                    )
+                ],
+                out_specs=[pl.BlockSpec((32, PER_STEP, 16, LANES), lambda i: (0, i, 0, 0))],
+            )(x_ref, o_ref)
+
+
+def pack(turn, parity, background, chunks, previous=(), after=()):
+    anywhere = pl.BlockSpec(memory_space=pl.ANY)
+    firsts = [sum(CHUNKS[:n]) for n in chunks]
+    ranges = tuple((f, CHUNKS[n]) for f, n in zip(firsts, chunks))
+    return pl.pallas_call(
+        functools.partial(pack_kernel, turn, ranges),
+        out_shape=tuple(
+            jax.ShapeDtypeStruct(
+                (32, CHUNKS[n] + (3 if n == CARRIER else 0), 16, LANES), jnp.bfloat16
+            )
+            for n in chunks
+        ),
+        in_specs=[pl.BlockSpec(memory_space=pltpu.SMEM), anywhere]
+        + [anywhere] * (len(previous) + len(after)),
+        out_specs=(anywhere,) * len(chunks),
+        scratch_shapes=[pltpu.VMEM((8 * PER_STEP, 64, LANES), jnp.float32)],
+        input_output_aliases={2 + n: n for n in range(len(previous))},
+        compiler_params=pltpu.CompilerParams(vmem_limit_bytes=VMEM_LIMIT),
+        cost_estimate=relayout_cost(sum(count for _, count in ranges)),
+        name="pack",
+    )(parity, background, *previous, *after)
+
+
 def relayout_cost(count):
     return pl.CostEstimate(
         flops=count * 65536 * 40, bytes_accessed=count * 262144, transcendentals=0
     )
-
-
-def pack(background, first, count, extra):
-    base = first // PER_STEP
-    return pl.pallas_call(
-        functools.partial(pack_kernel, PER_STEP),
-        out_shape=jax.ShapeDtypeStruct((32, count + extra, 16, LANES), jnp.bfloat16),
-        grid=(count // PER_STEP,),
-        in_specs=[
-            pl.BlockSpec((MEM_DEV, 2 * PER_STEP, 8, 512), lambda i: (0, base + i, 0, 0))
-        ],
-        out_specs=pl.BlockSpec((32, PER_STEP, 16, LANES), lambda i: (0, i, 0, 0)),
-        scratch_shapes=[pltpu.VMEM((8 * PER_STEP, 64, LANES), jnp.float32)],
-        compiler_params=pltpu.CompilerParams(vmem_limit_bytes=VMEM_LIMIT),
-        cost_estimate=relayout_cost(count),
-        name="pack",
-    )(background)
 
 
 def unpack_kernel(per_step, x_ref, *rest):
@@ -347,11 +372,6 @@
     firsts = [sum(CHUNKS[:n]) for n in range(len(CHUNKS))]
     slots = obs_cell.shape[-1]
     members = 256
-    blocks = [
-        pack(background, f, c, 3 if n == CARRIER else 0)
-        for n, (f, c) in enumerate(zip(firsts, CHUNKS))
-    ]
-
     inside = (jnp.arange(slots, dtype=jnp.int32) < obs_count[0, 0]).astype(jnp.float32)
     weight = inside * obs_precision[0, 0] / (members - 1.0)
     own = jnp.stack(
@@ -363,6 +383,11 @@
         ]
     )
     info = exchange(jnp.broadcast_to(own[None], (32,) + own.shape))
+    parity = (1 - (lax.axis_index("tile") & 1)).astype(jnp.int32).reshape(1)
+    (lead,) = pack(0, parity, background, (2,))
+    lead, *rest = pack(1, parity, background, (2, 0, 1), (lead,), (info,))
+    rest = pack(0, parity, background, (0, 1), tuple(rest), (lead,))
+    blocks = [rest[0], rest[1], lead]
     blocks[CARRIER] = gather_obs(info, blocks)
     arrived = [exchange(b) for b in blocks]
     hx = arrived[CARRIER][:, CHUNKS[CARRIER] :]
@@ -399,6 +424,12 @@
         P("member", "tile", None),
     )
     out_specs = P("member", None, "tile", None)
-    return jax.shard_map(
+    mapped = jax.shard_map(
         per_device, mesh=mesh, in_specs=in_specs, out_specs=out_specs, check_vma=False
     )
+
+    def run(*args):
+        with jax.sharding.use_abstract_mesh(mesh.abstract_mesh):
+            return mapped(*args)
+
+    return run

time: 319 us -> 286 us (0.90)
  waiting for transfers between devices: 156 us -> 127 us
  blocking collectives: 52.4 us -> 42.8 us
  local copies, waits for them, and re-layouts: 7.16 us -> 10.6 us
  starting transfers between devices: 47.9 us -> 51.2 us
    all_to_all x6, waiting for transfers between devices: 153 us -> 124 us  [exchange(): lax.all_to_all(blocks, 'member', split_axis=0, concat_axis=0, tiled=True)]
    all_to_all x1, blocking collectives: 52.4 us -> 42.8 us  [exchange(): lax.all_to_all(blocks, 'member', split_axis=0, concat_axis=0, tiled=True)]
    all_to_all x6, starting transfers between devices: 38.3 us -> 41.6 us  [exchange(): lax.all_to_all(blocks, 'member', split_axis=0, concat_axis=0, tiled=True)]
    unnamed x18 -> x16, local copies, waits for them, and re-layouts: 5.73 us -> 8.12 us
  transfers between devices with their start and end apart: 10 -> 10, of which waited for: 7 -> 7; matrix products, arithmetic and copies ran while one was open for 0% -> 1% of each run, Pallas kernels for 15% -> 12%
where the time goes in v3:
time: 286 us; the launch traced here: 284 us
  waiting for transfers between devices  127 us (44%)
  starting transfers between devices  51.2 us (18%)
  Pallas kernels  50.1 us (18%)
  blocking collectives  42.8 us (15%)
  local copies, waits for them, and re-layouts  10.6 us (4%)
    all_to_all x6, waiting for transfers between devices, exchange(): lax.all_to_all(blocks, 'member', split_axis=0, concat_axis=0, tiled=True)  124 us
    all_to_all x1, blocking collectives, exchange(): lax.all_to_all(blocks, 'member', split_axis=0, concat_axis=0, tiled=True)  42.8 us
    all_to_all x6, starting transfers between devices, exchange(): lax.all_to_all(blocks, 'member', split_axis=0, concat_axis=0, tiled=True)  41.6 us
    pallas_call x3, Pallas kernels, unpack(): pl.pallas_call(functools.partial(unpack_kernel, PER_STEP), out_shape=jax....  13.6 us
    pallas_call x3, Pallas kernels, pack(): pl.pallas_call(functools.partial(pack_kernel, turn, ranges), out_shape=tu...  13.5 us
    pallas_call x1, Pallas kernels, tile_weights(): pl.pallas_call(weights_kernel, out_shape=(jax.ShapeDtypeStruct((2, 256, 2...  9.9 us
    unnamed x16, local copies, waits for them, and re-layouts  8.12 us
    pallas_call x1, Pallas kernels, gather_obs(): pl.pallas_call(functools.partial(gather_kernel, CHUNKS, tiles), out_shape...  7.7 us
  transfers between devices with their start and end apart: 10, of which 7 were waited for; matrix products, arithmetic and copies ran while one was open for 1% of the time, Pallas kernels for 12%

profile of v3, /device:TPU:8, one launch (start us, length us, event | category | flops | bytes accessed | tf_op | source)
XLA Modules:
  0.0 284.4 jit_solution(10918523728745234248)
XLA Ops:
  0.7 0.7 fusion
  1.3 0.7 convert_bitcast_fusion
  2.0 0.7 pad_maximum_fusion.1
  2.7 0.7 broadcast_in_dim.2
  3.4 11.3 %all-to-all-start = ((f32[32,4,256]{2,1,0:T(4,128)}), f32[32,4,256]{2,1,0:T(4,128)S(1)}, u32[]{:S(2)}, u32[]{:S(2)}) async-start(f32[32,4,256]{2,1,0:T(4,128)} %broadcast_in_dim.2), calls=%async_computation | async-start | bytes 262144 | tf_op jit(solution)/shard_map/all_to_all | solution.py:368
  14.8 10.4 %all-to-all-done.refs_1_.info_ref = f32[32,4,256]{2,1,0:T(4,128)S(1)} async-done(((f32[32,4,256]{2,1,0:T(4,128)}), f32[32,4,256]{2,1,0:T(4,128)S(1)}, u32[]{:S(2)}, u32[]{:S(2)}) %all-to-all-start) | async-done | bytes 131104 | tf_op jit(solution)/shard_map/all_to_all | solution.py:368
  25.2 13.4 %pack.4 = (bf16[32,8,16,128]{3,2,1,0:T(8,128)(2,1)}, bf16[32,20,16,128]{3,2,1,0:T(8,128)(2,1)}, bf16[32,15,16,128]{3,2,1,0:T(8,128)(2,1)S(1)}) custom-call(s32[1]{0:T(128)} %bitcast.parity_ref, bf16[8,80,8,512]{3,2,1,0:T(8,128)(2,1)} %x_ref.5, bf16[32,8,16,128]{3,2,1,0:T(8,128)(2,1)} %pack.3.refs_0_, ...), custom_call_target="tpu_custom_call", output_to_operand_aliasing={{0}: (2, {})} | custom-call | flops 104857600 | bytes 10485760 | tf_op jit(solution)/shard_map/pack/pallas_call | solution.py:92
  38.6 3.9 %all-to-all-start.1 = ((bf16[32,8,16,128]{3,2,1,0:T(8,128)(2,1)}), bf16[32,8,16,128]{3,2,1,0:T(8,128)(2,1)S(1)}, u32[]{:S(2)}, u32[]{:S(2)}) async-start(bf16[32,8,16,128]{3,2,1,0:T(8,128)(2,1)} %get-tuple-element.12.refs_2_), calls=%async_computation.1 | async-start | bytes 2097152 | tf_op jit(solution)/shard_map/all_to_all | solution.py:368
  42.6 7.7 %gather_obs.1 = bf16[32,15,16,128]{3,2,1,0:T(8,128)(2,1)S(1)} custom-call(f32[32,4,256]{2,1,0:T(4,128)S(1)} %all-to-all-done.refs_1_.info_ref, bf16[32,20,16,128]{3,2,1,0:T(8,128)(2,1)} %get-tuple-element.15.refs_0_, bf16[32,15,16,128]{3,2,1,0:T(8,128)(2,1)S(1)} %get-tuple-element.16.refs_1_, ...), custom_call_target="tpu_custom_call", output_to_operand_aliasing={{}: (2, {})} | custom-call | flops 1342177280 | bytes 6291456 | tf_op jit(solution)/shard_map/gather_obs/pallas_call | solution.py:200
  50.3 10.6 %all-to-all-done.1.x_ref = bf16[32,8,16,128]{3,2,1,0:T(8,128)(2,1)S(1)} async-done(((bf16[32,8,16,128]{3,2,1,0:T(8,128)(2,1)}), bf16[32,8,16,128]{3,2,1,0:T(8,128)(2,1)S(1)}, u32[]{:S(2)}, u32[]{:S(2)}) %all-to-all-start.1) | async-done | bytes 1048608 | tf_op jit(solution)/shard_map/all_to_all | solution.py:368
  60.9 0.0 copy-start.3
  60.9 42.8 %all_to_all.35.own.x_ref = bf16[32,15,16,128]{3,2,1,0:T(8,128)(2,1)} all-to-all(bf16[32,15,16,128]{3,2,1,0:T(8,128)(2,1)S(1)} %gather_obs.1), channel_id=1, replica_groups=mesh['member'=32,'tile'=8] {'member'}, dimensions={0} | all-to-all | bytes 3932160 | tf_op jit(solution)/shard_map/all_to_all | solution.py:368
  103.7 0.0 copy-done.3
  103.7 6.3 %all-to-all-start.5 = ((bf16[32,20,16,128]{3,2,1,0:T(8,128)(2,1)}), bf16[32,20,16,128]{3,2,1,0:T(8,128)(2,1)S(1)}, u32[]{:S(2)}, u32[]{:S(2)}) async-start(bf16[32,20,16,128]{3,2,1,0:T(8,128)(2,1)} %get-tuple-element.15.refs_0_), calls=%async_computation.5 | async-start | bytes 5242880 | tf_op jit(solution)/shard_map/all_to_all | solution.py:368
  110.0 1.8 slice.4
  111.8 1.9 collective-permute-start.1
  113.7 2.4 collective-permute-start
  116.2 3.2 %collective-permute-start.3 = (f32[3,4,256]{2,1,0:T(4,128)S(1)}, f32[3,4,256]{2,1,0:T(4,128)S(1)}, u32[]{:S(2)}, u32[]{:S(2)}) collective-permute-start(f32[3,4,256]{2,1,0:T(4,128)S(1)} %pad_maximum_fusion.own_info), channel_id=1, source_target_pairs={{1,0},{2,1},{3,2},{4,3},{5,4},{6,5},{7,6},{9,8},{10,9},{11,10},{12... | collective-permute-start | bytes 36872 | tf_op jit(solution)/shard_map/ppermute | solution.py:405
  119.4 2.1 collective-permute-start.2
  121.5 0.0 collective-permute-done.3.above_info
  121.5 2.9 %collective-permute-done.2.below_info = f32[3,4,256]{2,1,0:T(4,128)S(1)} collective-permute-done((f32[3,4,256]{2,1,0:T(4,128)S(1)}, f32[3,4,256]{2,1,0:T(4,128)S(1)}, u32[]{:S(2)}, u32[]{:S(2)}) %collective-permute-start.2) | collective-permute-done | bytes 12320 | tf_op jit(solution)/shard_map/ppermute | solution.py:405
  124.4 0.0 collective-permute-done.1.above
  124.4 0.0 collective-permute-done.below
  124.4 0.0 copy-start.6
  124.4 0.8 copy-done.6
  125.1 0.0 copy-start.1
  125.1 1.5 copy-done.1
  126.7 0.0 copy-start.7
  126.7 1.0 copy-done.7
  127.7 9.9 %tile_weights.1 = (bf16[2,256,256]{2,1,0:T(8,128)(2,1)S(1)}, f32[2,256,128]{2,1,0:T(8,128)S(1)}) custom-call(bf16[32,15,16,128]{3,2,1,0:T(8,128)(2,1)S(1)} %copy-done.1, bf16[32,3,16,128]{3,2,1,0:T(8,128)(2,1)S(1)} %copy-done.7, bf16[32,3,16,128]{3,2,1,0:T(8,128)(2,1)S(1)} %collective-permute-done.1.above, f32[3,4,256]{2,1,0:T(4,128)S(1)} %pad_maximum_fusion.own_info, ...), custom_call_target="tpu_custom_call" | custom-call | flops 5368709120 | bytes 3145728 | tf_op jit(solution)/shard_map/tile_weights/pallas_call | solution.py:305
  137.6 1.8 transform.4
  139.4 0.0 copy-start.2
  139.4 1.1 copy-done.2
  140.6 21.1 %all-to-all-done.5.x_ref = bf16[32,20,16,128]{3,2,1,0:T(8,128)(2,1)S(1)} async-done(((bf16[32,20,16,128]{3,2,1,0:T(8,128)(2,1)}), bf16[32,20,16,128]{3,2,1,0:T(8,128)(2,1)S(1)}, u32[]{:S(2)}, u32[]{:S(2)}) %all-to-all-start.5) | async-done | bytes 2621472 | tf_op jit(solution)/shard_map/all_to_all | solution.py:368
  161.6 6.3 %all-to-all-start.4 = ((bf16[32,12,16,128]{3,2,1,0:T(8,128)(2,1)}), bf16[32,12,16,128]{3,2,1,0:T(8,128)(2,1)}, u32[]{:S(2)}, u32[]{:S(2)}) async-start(bf16[32,12,16,128]{3,2,1,0:T(8,128)(2,1)} %copy-done.2), calls=%async_computation.4 | async-start | bytes 3145728 | tf_op jit(solution)/shard_map/all_to_all | solution.py:368
  168.0 2.6 transform.5
  170.5 0.0 copy-start
  170.6 1.5 copy-done
  172.0 26.4 %all-to-all-done.4.x_ref = bf16[32,12,16,128]{3,2,1,0:T(8,128)(2,1)} async-done(((bf16[32,12,16,128]{3,2,1,0:T(8,128)(2,1)}), bf16[32,12,16,128]{3,2,1,0:T(8,128)(2,1)}, u32[]{:S(2)}, u32[]{:S(2)}) %all-to-all-start.4) | async-done | bytes 1572896 | tf_op jit(solution)/shard_map/all_to_all | solution.py:368
  198.5 5.4 %all-to-all-start.6 = ((bf16[32,20,16,128]{3,2,1,0:T(8,128)(2,1)}), bf16[32,20,16,128]{3,2,1,0:T(8,128)(2,1)S(1)}, u32[]{:S(2)}, u32[]{:S(2)}) async-start(bf16[32,20,16,128]{3,2,1,0:T(8,128)(2,1)} %copy-done), calls=%async_computation.6 | async-start | bytes 5242880 | tf_op jit(solution)/shard_map/all_to_all | solution.py:368
  203.9 0.0 copy-start.4
  203.9 1.2 copy-done.4
  205.1 1.0 transform.3
  206.2 0.0 copy-start.5
  206.2 1.0 copy-done.5
  207.2 47.2 %all-to-all-done.6.x_ref = bf16[32,20,16,128]{3,2,1,0:T(8,128)(2,1)S(1)} async-done(((bf16[32,20,16,128]{3,2,1,0:T(8,128)(2,1)}), bf16[32,20,16,128]{3,2,1,0:T(8,128)(2,1)S(1)}, u32[]{:S(2)}, u32[]{:S(2)}) %all-to-all-start.6) | async-done | bytes 2621472 | tf_op jit(solution)/shard_map/all_to_all | solution.py:368
  254.3 8.3 %all-to-all-start.3 = ((bf16[32,8,16,128]{3,2,1,0:T(8,128)(2,1)}), bf16[32,8,16,128]{3,2,1,0:T(8,128)(2,1)}, u32[]{:S(2)}, u32[]{:S(2)}) async-start(bf16[32,8,16,128]{3,2,1,0:T(8,128)(2,1)} %copy-done.5), calls=%async_computation.3 | async-start | bytes 2097152 | tf_op jit(solution)/shard_map/all_to_all | solution.py:368
  262.6 5.3 %unpack.3.rest_0_ = bf16[8,80,8,512]{3,2,1,0:T(8,128)(2,1)} custom-call(bf16[32,20,16,128]{3,2,1,0:T(8,128)(2,1)S(1)} %all-to-all-done.6.x_ref), custom_call_target="tpu_custom_call" | custom-call | flops 52428800 | bytes 5242880 | tf_op jit(solution)/shard_map/unpack/pallas_call | solution.py:147
  267.9 4.7 %unpack.4.rest_0_ = bf16[8,80,8,512]{3,2,1,0:T(8,128)(2,1)} custom-call(bf16[32,12,16,128]{3,2,1,0:T(8,128)(2,1)} %all-to-all-done.4.x_ref, bf16[8,80,8,512]{3,2,1,0:T(8,128)(2,1)} %unpack.3.rest_0_), custom_call_target="tpu_custom_call", output_to_operand_aliasing={{}: (1, {})} | custom-call | flops 31457280 | bytes 3145728 | tf_op jit(solution)/shard_map/unpack/pallas_call | solution.py:147
  272.6 8.3 %all-to-all-done.3.x_ref = bf16[32,8,16,128]{3,2,1,0:T(8,128)(2,1)} async-done(((bf16[32,8,16,128]{3,2,1,0:T(8,128)(2,1)}), bf16[32,8,16,128]{3,2,1,0:T(8,128)(2,1)}, u32[]{:S(2)}, u32[]{:S(2)}) %all-to-all-start.3) | async-done | bytes 1048608 | tf_op jit(solution)/shard_map/all_to_all | solution.py:368
  280.9 3.5 %unpack.5 = bf16[8,80,8,512]{3,2,1,0:T(8,128)(2,1)} custom-call(bf16[32,8,16,128]{3,2,1,0:T(8,128)(2,1)} %all-to-all-done.3.x_ref, bf16[8,80,8,512]{3,2,1,0:T(8,128)(2,1)} %unpack.4.rest_0_), custom_call_target="tpu_custom_call", output_to_operand_aliasing={{}: (1, {})} | custom-call | flops 20971520 | bytes 2097152 | tf_op jit(solution)/shard_map/unpack/pallas_call | solution.py:147
  (4 shorter events, 0.0 us)
Async XLA Ops:
  3.4 21.8 %all-to-all-start = ((f32[32,4,256]{2,1,0:T(4,128)}), f32[32,4,256]{2,1,0:T(4,128)S(1)}, u32[]{:S(2)}, u32[]{:S(2)}) async-start(f32[32,4,256]{2,1,0:T(4,128)} %broadcast_in_dim.2), calls=%async_computation | async-start | bytes 262144 | tf_op jit(solution)/shard_map/all_to_all | solution.py:368
  38.6 22.3 %all-to-all-start.1 = ((bf16[32,8,16,128]{3,2,1,0:T(8,128)(2,1)}), bf16[32,8,16,128]{3,2,1,0:T(8,128)(2,1)S(1)}, u32[]{:S(2)}, u32[]{:S(2)}) async-start(bf16[32,8,16,128]{3,2,1,0:T(8,128)(2,1)} %get-tuple-element.12.refs_2_), calls=%async_computation.1 | async-start | bytes 2097152 | tf_op jit(solution)/shard_map/all_to_all | solution.py:368
  60.9 42.8 %copy-start.3 = (bf16[32,8,16,128]{3,2,1,0:T(8,128)(2,1)}, bf16[32,8,16,128]{3,2,1,0:T(8,128)(2,1)S(1)}, u32[]{:S(2)}) copy-start(bf16[32,8,16,128]{3,2,1,0:T(8,128)(2,1)S(1)} %all-to-all-done.1.x_ref) | copy-start | bytes 3145732
  103.7 58.0 %all-to-all-start.5 = ((bf16[32,20,16,128]{3,2,1,0:T(8,128)(2,1)}), bf16[32,20,16,128]{3,2,1,0:T(8,128)(2,1)S(1)}, u32[]{:S(2)}, u32[]{:S(2)}) async-start(bf16[32,20,16,128]{3,2,1,0:T(8,128)(2,1)} %get-tuple-element.15.refs_0_), calls=%async_computation.5 | async-start | bytes 5242880 | tf_op jit(solution)/shard_map/all_to_all | solution.py:368
  111.8 12.6 %collective-permute-start.1 = (bf16[32,3,16,128]{3,2,1,0:T(8,128)(2,1)}, bf16[32,3,16,128]{3,2,1,0:T(8,128)(2,1)S(1)}, u32[]{:S(2)}, u32[]{:S(2)}) collective-permute-start(bf16[32,3,16,128]{3,2,1,0:T(8,128)(2,1)} %slice.4), channel_id=1, source_target_pairs={{1,0},{2,1},{3,2},{4,3},{5,4},{6,5},{7,6},{9,8},{10,9},{11,10},{12... | collective-permute-start | bytes 1179656 | tf_op jit(solution)/shard_map/ppermute | solution.py:404
  113.7 10.7 %collective-permute-start = (bf16[32,3,16,128]{3,2,1,0:T(8,128)(2,1)}, bf16[32,3,16,128]{3,2,1,0:T(8,128)(2,1)S(1)}, u32[]{:S(2)}, u32[]{:S(2)}) collective-permute-start(bf16[32,3,16,128]{3,2,1,0:T(8,128)(2,1)} %slice.4), channel_id=1, source_target_pairs={{0,1},{1,2},{2,3},{3,4},{4,5},{5,6},{6,7},{8,9},{9,10},{10,11},{11... | collective-permute-start | bytes 1179656 | tf_op jit(solution)/shard_map/ppermute | solution.py:404
  116.2 5.3 %collective-permute-start.3 = (f32[3,4,256]{2,1,0:T(4,128)S(1)}, f32[3,4,256]{2,1,0:T(4,128)S(1)}, u32[]{:S(2)}, u32[]{:S(2)}) collective-permute-start(f32[3,4,256]{2,1,0:T(4,128)S(1)} %pad_maximum_fusion.own_info), channel_id=1, source_target_pairs={{1,0},{2,1},{3,2},{4,3},{5,4},{6,5},{7,6},{9,8},{10,9},{11,10},{12... | collective-permute-start | bytes 36872 | tf_op jit(solution)/shard_map/ppermute | solution.py:405
  119.4 5.0 %collective-permute-start.2 = (f32[3,4,256]{2,1,0:T(4,128)S(1)}, f32[3,4,256]{2,1,0:T(4,128)S(1)}, u32[]{:S(2)}, u32[]{:S(2)}) collective-permute-start(f32[3,4,256]{2,1,0:T(4,128)S(1)} %pad_maximum_fusion.own_info), channel_id=1, source_target_pairs={{0,1},{1,2},{2,3},{3,4},{4,5},{5,6},{6,7},{8,9},{9,10},{10,11},{11... | collective-permute-start | bytes 36872 | tf_op jit(solution)/shard_map/ppermute | solution.py:405
  124.4 0.8 copy-start.6
  125.1 1.5 copy-start.1
  126.7 1.0 copy-start.7
  139.4 1.1 copy-start.2
  161.6 36.8 %all-to-all-start.4 = ((bf16[32,12,16,128]{3,2,1,0:T(8,128)(2,1)}), bf16[32,12,16,128]{3,2,1,0:T(8,128)(2,1)}, u32[]{:S(2)}, u32[]{:S(2)}) async-start(bf16[32,12,16,128]{3,2,1,0:T(8,128)(2,1)} %copy-done.2), calls=%async_computation.4 | async-start | bytes 3145728 | tf_op jit(solution)/shard_map/all_to_all | solution.py:368
  170.5 1.5 copy-start
  198.5 55.9 %all-to-all-start.6 = ((bf16[32,20,16,128]{3,2,1,0:T(8,128)(2,1)}), bf16[32,20,16,128]{3,2,1,0:T(8,128)(2,1)S(1)}, u32[]{:S(2)}, u32[]{:S(2)}) async-start(bf16[32,20,16,128]{3,2,1,0:T(8,128)(2,1)} %copy-done), calls=%async_computation.6 | async-start | bytes 5242880 | tf_op jit(solution)/shard_map/all_to_all | solution.py:368
  203.9 1.2 copy-start.4
  206.2 1.0 copy-start.5
  254.3 26.6 %all-to-all-start.3 = ((bf16[32,8,16,128]{3,2,1,0:T(8,128)(2,1)}), bf16[32,8,16,128]{3,2,1,0:T(8,128)(2,1)}, u32[]{:S(2)}, u32[]{:S(2)}) async-start(bf16[32,8,16,128]{3,2,1,0:T(8,128)(2,1)} %copy-done.5), calls=%async_computation.3 | async-start | bytes 2097152 | tf_op jit(solution)/shard_map/all_to_all | solution.py:368

commit v4 on v3

--- a/solution.py
+++ b/solution.py
@@ -328,7 +328,8 @@
     )(*values, *infos)
 
 
-def transform_kernel(per_step, x_ref, w_ref, keep_ref, o_ref):
+def transform_kernel(per_step, x_ref, w_ref, keep_ref, *rest):
+    o_ref = rest[-1]
     for b in range(per_step):
         both = x_ref[:, b].astype(jnp.float32).reshape(32, 2, MEM_DEV, LANES)
         outs = []
@@ -344,24 +345,27 @@
         o_ref[:, b] = result.astype(jnp.bfloat16)
 
 
-def transform(blocks, count, weights, keep, per_step):
+def transform(blocks, count, weights, keep, per_step, total, first=0, previous=()):
+    base = first // per_step
     spec = pl.BlockSpec((32, per_step, 16, LANES), lambda i: (0, i, 0, 0))
     return pl.pallas_call(
         functools.partial(transform_kernel, per_step),
-        out_shape=jax.ShapeDtypeStruct((32, count, 16, LANES), jnp.bfloat16),
+        out_shape=jax.ShapeDtypeStruct((32, total, 16, LANES), jnp.bfloat16),
         grid=(count // per_step,),
         in_specs=[
             spec,
             pl.BlockSpec((2, 256, 256), lambda i: (0, 0, 0)),
             pl.BlockSpec((2, 256, LANES), lambda i: (0, 0, 0)),
-        ],
-        out_specs=spec,
+        ]
+        + [pl.BlockSpec(memory_space=pl.ANY)] * len(previous),
+        out_specs=pl.BlockSpec((32, per_step, 16, LANES), lambda i: (0, base + i, 0, 0)),
+        input_output_aliases={3: 0} if previous else {},
         compiler_params=pltpu.CompilerParams(vmem_limit_bytes=VMEM_LIMIT),
         cost_estimate=pl.CostEstimate(
             flops=count * 4 * 256 * 256 * 128, bytes_accessed=count * 262144, transcendentals=0
         ),
         name="transform",
-    )(blocks, weights, keep)
+    )(blocks, weights, keep, *previous)
 
 
 def exchange(blocks):
@@ -369,7 +373,6 @@
 
 
 def per_device(background, obs_cell, obs_channel, obs_count, obs_value, obs_precision):
-    firsts = [sum(CHUNKS[:n]) for n in range(len(CHUNKS))]
     slots = obs_cell.shape[-1]
     members = 256
     inside = (jnp.arange(slots, dtype=jnp.int32) < obs_count[0, 0]).astype(jnp.float32)
@@ -405,13 +408,12 @@
     infos = (near, lax.ppermute(near, "tile", up), lax.ppermute(near, "tile", down))
     weights, keep = tile_weights(values, infos)
 
-    back = [
-        exchange(transform(b, c, weights, keep, 4)) for b, c in zip(arrived, CHUNKS)
-    ]
-    out = None
-    for b, f, c in zip(back, firsts, CHUNKS):
-        out = unpack(b, out, f, c, background.shape)
-    return out
+    total = CHUNKS[1] + CHUNKS[2]
+    early = transform(arrived[2], CHUNKS[2], weights, keep, 4, total, CHUNKS[1])
+    early = transform(arrived[1], CHUNKS[1], weights, keep, 4, total, 0, (early,))
+    late = transform(arrived[0], CHUNKS[0], weights, keep, 4, CHUNKS[0])
+    out = unpack(exchange(early), None, CHUNKS[0], total, background.shape)
+    return unpack(exchange(late), out, 0, CHUNKS[0], background.shape)
 
 
 def solution(mesh):

time: 286 us -> 281 us (0.983)
  starting transfers between devices: 51.2 us -> 43.8 us
  local copies, waits for them, and re-layouts: 10.6 us -> 7.28 us
  Pallas kernels: 50.1 us -> 53.1 us
  waiting for transfers between devices: 127 us -> 130 us
    all_to_all x6 -> x5, starting transfers between devices: 41.6 us -> 34.2 us  [exchange(): lax.all_to_all(blocks, 'member', split_axis=0, concat_axis=0, tiled=True)]
    all_to_all x6 -> x5, waiting for transfers between devices: 124 us -> 128 us  [exchange(): lax.all_to_all(blocks, 'member', split_axis=0, concat_axis=0, tiled=True)]
    unnamed x16 -> x10, local copies, waits for them, and re-layouts: 8.12 us -> 4.82 us
    pallas_call x3, Pallas kernels: 5.45 us -> 8.37 us  [transform(): pl.pallas_call(functools.partial(transform_kernel, per_step), out_shape=j...]
    pallas_call x3 -> x2, Pallas kernels: 13.6 us -> 13.7 us  [unpack(): pl.pallas_call(functools.partial(unpack_kernel, PER_STEP), out_shape=jax....]
  transfers between devices with their start and end apart: 10 -> 9, of which waited for: 7 -> 6; matrix products, arithmetic and copies ran while one was open for 1% -> 1% of each run, Pallas kernels for 12% -> 12%
where the time goes in v4:
time: 281 us; the launch traced here: 280 us
  waiting for transfers between devices  130 us (46%)
  Pallas kernels  53.1 us (19%)
  starting transfers between devices  43.8 us (16%)
  blocking collectives  42.6 us (15%)
  local copies, waits for them, and re-layouts  7.28 us (3%)
    all_to_all x5, waiting for transfers between devices, exchange(): lax.all_to_all(blocks, 'member', split_axis=0, concat_axis=0, tiled=True)  128 us
    all_to_all x1, blocking collectives, exchange(): lax.all_to_all(blocks, 'member', split_axis=0, concat_axis=0, tiled=True)  42.6 us
    all_to_all x5, starting transfers between devices, exchange(): lax.all_to_all(blocks, 'member', split_axis=0, concat_axis=0, tiled=True)  34.2 us
    pallas_call x2, Pallas kernels, unpack(): pl.pallas_call(functools.partial(unpack_kernel, PER_STEP), out_shape=jax....  13.7 us
    pallas_call x3, Pallas kernels, pack(): pl.pallas_call(functools.partial(pack_kernel, turn, ranges), out_shape=tu...  13.4 us
    pallas_call x1, Pallas kernels, tile_weights(): pl.pallas_call(weights_kernel, out_shape=(jax.ShapeDtypeStruct((2, 256, 2...  9.9 us
    pallas_call x3, Pallas kernels, transform(): pl.pallas_call(functools.partial(transform_kernel, per_step), out_shape=j...  8.37 us
    pallas_call x1, Pallas kernels, gather_obs(): pl.pallas_call(functools.partial(gather_kernel, CHUNKS, tiles), out_shape...  7.7 us
  transfers between devices with their start and end apart: 9, of which 6 were waited for; matrix products, arithmetic and copies ran while one was open for 1% of the time, Pallas kernels for 12%

profile of v4, /device:TPU:8, one launch (start us, length us, event | category | flops | bytes accessed | tf_op | source)
XLA Modules:
  0.0 280.2 jit_solution(12868169032835029594)
XLA Ops:
  0.7 0.7 fusion
  1.3 0.7 convert_bitcast_fusion
  2.0 0.7 pad_maximum_fusion.1
  2.7 0.7 broadcast_in_dim.2
  3.4 11.3 %all-to-all-start = ((f32[32,4,256]{2,1,0:T(4,128)}), f32[32,4,256]{2,1,0:T(4,128)S(1)}, u32[]{:S(2)}, u32[]{:S(2)}) async-start(f32[32,4,256]{2,1,0:T(4,128)} %broadcast_in_dim.2), calls=%async_computation | async-start | bytes 262144 | tf_op jit(solution)/shard_map/all_to_all | solution.py:372
  14.8 10.4 %all-to-all-done.refs_1_.info_ref = f32[32,4,256]{2,1,0:T(4,128)S(1)} async-done(((f32[32,4,256]{2,1,0:T(4,128)}), f32[32,4,256]{2,1,0:T(4,128)S(1)}, u32[]{:S(2)}, u32[]{:S(2)}) %all-to-all-start) | async-done | bytes 131104 | tf_op jit(solution)/shard_map/all_to_all | solution.py:372
  25.2 13.4 %pack.4 = (bf16[32,8,16,128]{3,2,1,0:T(8,128)(2,1)}, bf16[32,20,16,128]{3,2,1,0:T(8,128)(2,1)}, bf16[32,15,16,128]{3,2,1,0:T(8,128)(2,1)S(1)}) custom-call(s32[1]{0:T(128)} %bitcast.parity_ref, bf16[8,80,8,512]{3,2,1,0:T(8,128)(2,1)} %x_ref.5, bf16[32,8,16,128]{3,2,1,0:T(8,128)(2,1)} %pack.3.refs_0_, ...), custom_call_target="tpu_custom_call", output_to_operand_aliasing={{0}: (2, {})} | custom-call | flops 104857600 | bytes 10485760 | tf_op jit(solution)/shard_map/pack/pallas_call | solution.py:92
  38.6 4.7 %all-to-all-start.4 = ((bf16[32,8,16,128]{3,2,1,0:T(8,128)(2,1)}), bf16[32,8,16,128]{3,2,1,0:T(8,128)(2,1)}, u32[]{:S(2)}, u32[]{:S(2)}) async-start(bf16[32,8,16,128]{3,2,1,0:T(8,128)(2,1)} %get-tuple-element.14.refs_2_), calls=%async_computation.4 | async-start | bytes 2097152 | tf_op jit(solution)/shard_map/all_to_all | solution.py:372
  43.3 7.7 %gather_obs.1 = bf16[32,15,16,128]{3,2,1,0:T(8,128)(2,1)S(1)} custom-call(f32[32,4,256]{2,1,0:T(4,128)S(1)} %all-to-all-done.refs_1_.info_ref, bf16[32,20,16,128]{3,2,1,0:T(8,128)(2,1)} %get-tuple-element.15.refs_0_, bf16[32,15,16,128]{3,2,1,0:T(8,128)(2,1)S(1)} %get-tuple-element.16.refs_1_, ...), custom_call_target="tpu_custom_call", output_to_operand_aliasing={{}: (2, {})} | custom-call | flops 1342177280 | bytes 6291456 | tf_op jit(solution)/shard_map/gather_obs/pallas_call | solution.py:200
  51.0 10.6 %all-to-all-done.4.x_ref = bf16[32,8,16,128]{3,2,1,0:T(8,128)(2,1)} async-done(((bf16[32,8,16,128]{3,2,1,0:T(8,128)(2,1)}), bf16[32,8,16,128]{3,2,1,0:T(8,128)(2,1)}, u32[]{:S(2)}, u32[]{:S(2)}) %all-to-all-start.4) | async-done | bytes 1048608 | tf_op jit(solution)/shard_map/all_to_all | solution.py:372
  61.6 42.6 %all_to_all.30.own.x_ref = bf16[32,15,16,128]{3,2,1,0:T(8,128)(2,1)} all-to-all(bf16[32,15,16,128]{3,2,1,0:T(8,128)(2,1)S(1)} %gather_obs.1), channel_id=1, replica_groups=mesh['member'=32,'tile'=8] {'member'}, dimensions={0} | all-to-all | bytes 3932160 | tf_op jit(solution)/shard_map/all_to_all | solution.py:372
  104.2 6.1 %all-to-all-start.1 = ((bf16[32,20,16,128]{3,2,1,0:T(8,128)(2,1)}), bf16[32,20,16,128]{3,2,1,0:T(8,128)(2,1)S(1)}, u32[]{:S(2)}, u32[]{:S(2)}) async-start(bf16[32,20,16,128]{3,2,1,0:T(8,128)(2,1)} %get-tuple-element.15.refs_0_), calls=%async_computation.1 | async-start | bytes 5242880 | tf_op jit(solution)/shard_map/all_to_all | solution.py:372
  110.3 1.8 slice.4
  112.1 1.9 collective-permute-start.1
  114.0 2.4 collective-permute-start
  116.5 3.2 %collective-permute-start.3 = (f32[3,4,256]{2,1,0:T(4,128)S(1)}, f32[3,4,256]{2,1,0:T(4,128)S(1)}, u32[]{:S(2)}, u32[]{:S(2)}) collective-permute-start(f32[3,4,256]{2,1,0:T(4,128)S(1)} %pad_maximum_fusion.own_info), channel_id=1, source_target_pairs={{1,0},{2,1},{3,2},{4,3},{5,4},{6,5},{7,6},{9,8},{10,9},{11,10},{12... | collective-permute-start | bytes 36872 | tf_op jit(solution)/shard_map/ppermute | solution.py:408
  119.6 2.1 collective-permute-start.2
  121.7 0.0 collective-permute-done.3.above_info
  121.8 2.9 %collective-permute-done.2.below_info = f32[3,4,256]{2,1,0:T(4,128)S(1)} collective-permute-done((f32[3,4,256]{2,1,0:T(4,128)S(1)}, f32[3,4,256]{2,1,0:T(4,128)S(1)}, u32[]{:S(2)}, u32[]{:S(2)}) %collective-permute-start.2) | collective-permute-done | bytes 12320 | tf_op jit(solution)/shard_map/ppermute | solution.py:408
  124.6 0.0 collective-permute-done.1.above
  124.7 0.0 collective-permute-done.below
  124.7 0.0 copy-start.3
  124.7 0.7 copy-done.3
  125.4 0.0 copy-start.1
  125.4 1.5 copy-done.1
  126.9 0.0 copy-start.4
  127.0 1.0 copy-done.4
  127.9 9.9 %tile_weights.1 = (bf16[2,256,256]{2,1,0:T(8,128)(2,1)S(1)}, f32[2,256,128]{2,1,0:T(8,128)S(1)}) custom-call(bf16[32,15,16,128]{3,2,1,0:T(8,128)(2,1)S(1)} %copy-done.1, bf16[32,3,16,128]{3,2,1,0:T(8,128)(2,1)S(1)} %copy-done.4, bf16[32,3,16,128]{3,2,1,0:T(8,128)(2,1)S(1)} %collective-permute-done.1.above, f32[3,4,256]{2,1,0:T(4,128)S(1)} %pad_maximum_fusion.own_info, ...), custom_call_target="tpu_custom_call" | custom-call | flops 5368709120 | bytes 3145728 | tf_op jit(solution)/shard_map/tile_weights/pallas_call | solution.py:305
  137.9 0.0 copy-start.2
  137.9 3.0 %transform.4.rest_0_ = bf16[32,20,16,128]{3,2,1,0:T(8,128)(2,1)} custom-call(bf16[32,8,16,128]{3,2,1,0:T(8,128)(2,1)} %all-to-all-done.4.x_ref, bf16[2,256,256]{2,1,0:T(8,128)(2,1)S(1)} %get-tuple-element.17.w_ref, f32[2,256,128]{2,1,0:T(8,128)S(1)} %get-tuple-element.18.keep_ref), custom_call_target="tpu_custom_call" | custom-call | flops 268435456 | bytes 2097152 | tf_op jit(solution)/shard_map/transform/pallas_call | solution.py:351
  140.8 0.0 copy-done.2
  140.8 2.8 %transform.5 = bf16[32,20,16,128]{3,2,1,0:T(8,128)(2,1)} custom-call(bf16[32,15,16,128]{3,2,1,0:T(8,128)(2,1)S(1)} %copy-done.2, bf16[2,256,256]{2,1,0:T(8,128)(2,1)S(1)} %get-tuple-element.17.w_ref, f32[2,256,128]{2,1,0:T(8,128)S(1)} %get-tuple-element.18.keep_ref, bf16[32,20,16,128]{3,2,1,0:T(8,128)(2,1)} %transform.4.rest_0_), custom_call_target="tpu_custom_call", output_to_operand_aliasing={{}: (3, {})} | custom-call | flops 402653184 | bytes 3145728 | tf_op jit(solution)/shard_map/transform/pallas_call | solution.py:351
  143.7 16.3 %all-to-all-done.1.x_ref = bf16[32,20,16,128]{3,2,1,0:T(8,128)(2,1)S(1)} async-done(((bf16[32,20,16,128]{3,2,1,0:T(8,128)(2,1)}), bf16[32,20,16,128]{3,2,1,0:T(8,128)(2,1)S(1)}, u32[]{:S(2)}, u32[]{:S(2)}) %all-to-all-start.1) | async-done | bytes 2621472 | tf_op jit(solution)/shard_map/all_to_all | solution.py:372
  160.0 6.3 %all-to-all-start.5 = ((bf16[32,20,16,128]{3,2,1,0:T(8,128)(2,1)}), bf16[32,20,16,128]{3,2,1,0:T(8,128)(2,1)}, u32[]{:S(2)}, u32[]{:S(2)}) async-start(bf16[32,20,16,128]{3,2,1,0:T(8,128)(2,1)} %transform.5), calls=%async_computation.5 | async-start | bytes 5242880 | tf_op jit(solution)/shard_map/all_to_all | solution.py:372
  166.3 2.6 transform.3
  168.9 0.0 copy-start
  168.9 1.5 copy-done
  170.4 46.1 %all-to-all-done.5.x_ref = bf16[32,20,16,128]{3,2,1,0:T(8,128)(2,1)} async-done(((bf16[32,20,16,128]{3,2,1,0:T(8,128)(2,1)}), bf16[32,20,16,128]{3,2,1,0:T(8,128)(2,1)}, u32[]{:S(2)}, u32[]{:S(2)}) %all-to-all-start.5) | async-done | bytes 2621472 | tf_op jit(solution)/shard_map/all_to_all | solution.py:372
  216.5 5.8 %all-to-all-start.3 = ((bf16[32,20,16,128]{3,2,1,0:T(8,128)(2,1)}), bf16[32,20,16,128]{3,2,1,0:T(8,128)(2,1)}, u32[]{:S(2)}, u32[]{:S(2)}) async-start(bf16[32,20,16,128]{3,2,1,0:T(8,128)(2,1)} %copy-done), calls=%async_computation.3 | async-start | bytes 5242880 | tf_op jit(solution)/shard_map/all_to_all | solution.py:372
  222.3 6.9 %unpack.2.rest_0_ = bf16[8,80,8,512]{3,2,1,0:T(8,128)(2,1)} custom-call(bf16[32,20,16,128]{3,2,1,0:T(8,128)(2,1)} %all-to-all-done.5.x_ref), custom_call_target="tpu_custom_call" | custom-call | flops 52428800 | bytes 5242880 | tf_op jit(solution)/shard_map/unpack/pallas_call | solution.py:147
  229.1 44.2 %all-to-all-done.3.x_ref = bf16[32,20,16,128]{3,2,1,0:T(8,128)(2,1)} async-done(((bf16[32,20,16,128]{3,2,1,0:T(8,128)(2,1)}), bf16[32,20,16,128]{3,2,1,0:T(8,128)(2,1)}, u32[]{:S(2)}, u32[]{:S(2)}) %all-to-all-start.3) | async-done | bytes 2621472 | tf_op jit(solution)/shard_map/all_to_all | solution.py:372
  273.3 6.8 %unpack.3 = bf16[8,80,8,512]{3,2,1,0:T(8,128)(2,1)} custom-call(bf16[32,20,16,128]{3,2,1,0:T(8,128)(2,1)} %all-to-all-done.3.x_ref, bf16[8,80,8,512]{3,2,1,0:T(8,128)(2,1)} %unpack.2.rest_0_), custom_call_target="tpu_custom_call", output_to_operand_aliasing={{}: (1, {})} | custom-call | flops 52428800 | bytes 5242880 | tf_op jit(solution)/shard_map/unpack/pallas_call | solution.py:147
  (4 shorter events, 0.0 us)
Async XLA Ops:
  3.4 21.8 %all-to-all-start = ((f32[32,4,256]{2,1,0:T(4,128)}), f32[32,4,256]{2,1,0:T(4,128)S(1)}, u32[]{:S(2)}, u32[]{:S(2)}) async-start(f32[32,4,256]{2,1,0:T(4,128)} %broadcast_in_dim.2), calls=%async_computation | async-start | bytes 262144 | tf_op jit(solution)/shard_map/all_to_all | solution.py:372
  38.6 23.0 %all-to-all-start.4 = ((bf16[32,8,16,128]{3,2,1,0:T(8,128)(2,1)}), bf16[32,8,16,128]{3,2,1,0:T(8,128)(2,1)}, u32[]{:S(2)}, u32[]{:S(2)}) async-start(bf16[32,8,16,128]{3,2,1,0:T(8,128)(2,1)} %get-tuple-element.14.refs_2_), calls=%async_computation.4 | async-start | bytes 2097152 | tf_op jit(solution)/shard_map/all_to_all | solution.py:372
  104.2 55.8 %all-to-all-start.1 = ((bf16[32,20,16,128]{3,2,1,0:T(8,128)(2,1)}), bf16[32,20,16,128]{3,2,1,0:T(8,128)(2,1)S(1)}, u32[]{:S(2)}, u32[]{:S(2)}) async-start(bf16[32,20,16,128]{3,2,1,0:T(8,128)(2,1)} %get-tuple-element.15.refs_0_), calls=%async_computation.1 | async-start | bytes 5242880 | tf_op jit(solution)/shard_map/all_to_all | solution.py:372
  112.1 12.6 %collective-permute-start.1 = (bf16[32,3,16,128]{3,2,1,0:T(8,128)(2,1)}, bf16[32,3,16,128]{3,2,1,0:T(8,128)(2,1)S(1)}, u32[]{:S(2)}, u32[]{:S(2)}) collective-permute-start(bf16[32,3,16,128]{3,2,1,0:T(8,128)(2,1)} %slice.4), channel_id=1, source_target_pairs={{1,0},{2,1},{3,2},{4,3},{5,4},{6,5},{7,6},{9,8},{10,9},{11,10},{12... | collective-permute-start | bytes 1179656 | tf_op jit(solution)/shard_map/ppermute | solution.py:407
  114.0 10.7 %collective-permute-start = (bf16[32,3,16,128]{3,2,1,0:T(8,128)(2,1)}, bf16[32,3,16,128]{3,2,1,0:T(8,128)(2,1)S(1)}, u32[]{:S(2)}, u32[]{:S(2)}) collective-permute-start(bf16[32,3,16,128]{3,2,1,0:T(8,128)(2,1)} %slice.4), channel_id=1, source_target_pairs={{0,1},{1,2},{2,3},{3,4},{4,5},{5,6},{6,7},{8,9},{9,10},{10,11},{11... | collective-permute-start | bytes 1179656 | tf_op jit(solution)/shard_map/ppermute | solution.py:407
  116.5 5.3 %collective-permute-start.3 = (f32[3,4,256]{2,1,0:T(4,128)S(1)}, f32[3,4,256]{2,1,0:T(4,128)S(1)}, u32[]{:S(2)}, u32[]{:S(2)}) collective-permute-start(f32[3,4,256]{2,1,0:T(4,128)S(1)} %pad_maximum_fusion.own_info), channel_id=1, source_target_pairs={{1,0},{2,1},{3,2},{4,3},{5,4},{6,5},{7,6},{9,8},{10,9},{11,10},{12... | collective-permute-start | bytes 36872 | tf_op jit(solution)/shard_map/ppermute | solution.py:408
  119.6 5.0 %collective-permute-start.2 = (f32[3,4,256]{2,1,0:T(4,128)S(1)}, f32[3,4,256]{2,1,0:T(4,128)S(1)}, u32[]{:S(2)}, u32[]{:S(2)}) collective-permute-start(f32[3,4,256]{2,1,0:T(4,128)S(1)} %pad_maximum_fusion.own_info), channel_id=1, source_target_pairs={{0,1},{1,2},{2,3},{3,4},{4,5},{5,6},{6,7},{8,9},{9,10},{10,11},{11... | collective-permute-start | bytes 36872 | tf_op jit(solution)/shard_map/ppermute | solution.py:408
  124.7 0.7 copy-start.3
  125.4 1.5 copy-start.1
  126.9 1.0 copy-start.4
  137.9 3.0 %copy-start.2 = (bf16[32,15,16,128]{3,2,1,0:T(8,128)(2,1)S(1)}, bf16[32,15,16,128]{3,2,1,0:T(8,128)(2,1)}, u32[]{:S(2)}) copy-start(bf16[32,15,16,128]{3,2,1,0:T(8,128)(2,1)} %all_to_all.30.own.x_ref) | copy-start | bytes 5898244
  160.0 56.5 %all-to-all-start.5 = ((bf16[32,20,16,128]{3,2,1,0:T(8,128)(2,1)}), bf16[32,20,16,128]{3,2,1,0:T(8,128)(2,1)}, u32[]{:S(2)}, u32[]{:S(2)}) async-start(bf16[32,20,16,128]{3,2,1,0:T(8,128)(2,1)} %transform.5), calls=%async_computation.5 | async-start | bytes 5242880 | tf_op jit(solution)/shard_map/all_to_all | solution.py:372
  168.9 1.5 copy-start
  216.5 56.8 %all-to-all-start.3 = ((bf16[32,20,16,128]{3,2,1,0:T(8,128)(2,1)}), bf16[32,20,16,128]{3,2,1,0:T(8,128)(2,1)}, u32[]{:S(2)}, u32[]{:S(2)}) async-start(bf16[32,20,16,128]{3,2,1,0:T(8,128)(2,1)} %copy-done), calls=%async_computation.3 | async-start | bytes 5242880 | tf_op jit(solution)/shard_map/all_to_all | solution.py:372

commit v5 on v4

--- a/solution.py
+++ b/solution.py
@@ -368,24 +368,39 @@
     )(blocks, weights, keep, *previous)
 
 
+def slot_rows_kernel(count_ref, cell_ref, channel_ref, value_ref, precision_ref, o_ref):
+    shape = (1, 256)
+    inside = lax.broadcasted_iota(jnp.int32, shape, 1) < count_ref[0, 0]
+    weight = inside.astype(jnp.float32) * precision_ref[0] / 255.0
+    rows = (
+        cell_ref[0].astype(jnp.float32),
+        channel_ref[0].astype(jnp.float32),
+        value_ref[0],
+        weight,
+    )
+    for n, row in enumerate(rows):
+        o_ref[:, n : n + 1] = jnp.broadcast_to(row[None], (32, 1, 256))
+
+
+def slot_rows(count, *rows):
+    vmem = pl.BlockSpec(memory_space=pltpu.VMEM)
+    return pl.pallas_call(
+        slot_rows_kernel,
+        out_shape=jax.ShapeDtypeStruct((32, 4, 256), jnp.float32),
+        in_specs=[pl.BlockSpec(memory_space=pltpu.SMEM)] + [vmem] * 4,
+        out_specs=vmem,
+        name="slot_rows",
+    )(count, *rows)
+
+
 def exchange(blocks):
     return lax.all_to_all(blocks, "member", split_axis=0, concat_axis=0, tiled=True)
 
 
 def per_device(background, obs_cell, obs_channel, obs_count, obs_value, obs_precision):
-    slots = obs_cell.shape[-1]
-    members = 256
-    inside = (jnp.arange(slots, dtype=jnp.int32) < obs_count[0, 0]).astype(jnp.float32)
-    weight = inside * obs_precision[0, 0] / (members - 1.0)
-    own = jnp.stack(
-        [
-            obs_cell[0, 0].astype(jnp.float32),
-            obs_channel[0, 0].astype(jnp.float32),
-            obs_value[0, 0],
-            weight,
-        ]
-    )
-    info = exchange(jnp.broadcast_to(own[None], (32,) + own.shape))
+    info = exchange(
+        slot_rows(obs_count, obs_cell, obs_channel, obs_value, obs_precision)
+    )
     parity = (1 - (lax.axis_index("tile") & 1)).astype(jnp.int32).reshape(1)
     (lead,) = pack(0, parity, background, (2,))
     lead, *rest = pack(1, parity, background, (2, 0, 1), (lead,), (info,))

time: 281 us -> 280 us (level)
  no operation moved by 1% of the time
where the time goes in v5:
time: 280 us; the launch traced here: 278 us
  waiting for transfers between devices  128 us (46%)
  Pallas kernels  54.5 us (19%)
  starting transfers between devices  45.3 us (16%)
  blocking collectives  42.6 us (15%)
  local copies, waits for them, and re-layouts  6.62 us (2%)
    all_to_all x5, waiting for transfers between devices, exchange(): lax.all_to_all(blocks, 'member', split_axis=0, concat_axis=0, tiled=True)  125 us
    all_to_all x1, blocking collectives, exchange(): lax.all_to_all(blocks, 'member', split_axis=0, concat_axis=0, tiled=True)  42.6 us
    all_to_all x5, starting transfers between devices, exchange(): lax.all_to_all(blocks, 'member', split_axis=0, concat_axis=0, tiled=True)  35.7 us
    pallas_call x2, Pallas kernels, unpack(): pl.pallas_call(functools.partial(unpack_kernel, PER_STEP), out_shape=jax....  13.7 us
    pallas_call x3, Pallas kernels, pack(): pl.pallas_call(functools.partial(pack_kernel, turn, ranges), out_shape=tu...  13.5 us
    pallas_call x1, Pallas kernels, tile_weights(): pl.pallas_call(weights_kernel, out_shape=(jax.ShapeDtypeStruct((2, 256, 2...  9.9 us
    pallas_call x3, Pallas kernels, transform(): pl.pallas_call(functools.partial(transform_kernel, per_step), out_shape=j...  8.38 us
    pallas_call x1, Pallas kernels, gather_obs(): pl.pallas_call(functools.partial(gather_kernel, CHUNKS, tiles), out_shape...  7.7 us
  transfers between devices with their start and end apart: 9, of which 6 were waited for; matrix products, arithmetic and copies ran while one was open for 1% of the time, Pallas kernels for 12%

profile of v5, /device:TPU:8, one launch (start us, length us, event | category | flops | bytes accessed | tf_op | source)
XLA Modules:
  0.0 278.3 jit_solution(11969397155174875925)
XLA Ops:
  0.7 1.4 slot_rows.1
  2.1 11.3 %all-to-all-start = ((f32[32,4,256]{2,1,0:T(4,128)}), f32[32,4,256]{2,1,0:T(4,128)S(1)}, u32[]{:S(2)}, u32[]{:S(2)}) async-start(f32[32,4,256]{2,1,0:T(4,128)} %slot_rows.1), calls=%async_computation | async-start | bytes 262144 | tf_op jit(solution)/shard_map/all_to_all | solution.py:397
  13.4 10.4 %all-to-all-done.refs_1_.info_ref = f32[32,4,256]{2,1,0:T(4,128)S(1)} async-done(((f32[32,4,256]{2,1,0:T(4,128)}), f32[32,4,256]{2,1,0:T(4,128)S(1)}, u32[]{:S(2)}, u32[]{:S(2)}) %all-to-all-start) | async-done | bytes 131104 | tf_op jit(solution)/shard_map/all_to_all | solution.py:397
  23.8 13.4 %pack.4 = (bf16[32,8,16,128]{3,2,1,0:T(8,128)(2,1)}, bf16[32,20,16,128]{3,2,1,0:T(8,128)(2,1)}, bf16[32,15,16,128]{3,2,1,0:T(8,128)(2,1)S(1)}) custom-call(s32[1]{0:T(128)} %bitcast.parity_ref, bf16[8,80,8,512]{3,2,1,0:T(8,128)(2,1)} %x_ref.5, bf16[32,8,16,128]{3,2,1,0:T(8,128)(2,1)} %pack.3.refs_0_, ...), custom_call_target="tpu_custom_call", output_to_operand_aliasing={{0}: (2, {})} | custom-call | flops 104857600 | bytes 10485760 | tf_op jit(solution)/shard_map/pack/pallas_call | solution.py:92
  37.3 4.7 %all-to-all-start.4 = ((bf16[32,8,16,128]{3,2,1,0:T(8,128)(2,1)}), bf16[32,8,16,128]{3,2,1,0:T(8,128)(2,1)}, u32[]{:S(2)}, u32[]{:S(2)}) async-start(bf16[32,8,16,128]{3,2,1,0:T(8,128)(2,1)} %get-tuple-element.14.refs_2_), calls=%async_computation.4 | async-start | bytes 2097152 | tf_op jit(solution)/shard_map/all_to_all | solution.py:397
  42.0 7.7 %gather_obs.1 = bf16[32,15,16,128]{3,2,1,0:T(8,128)(2,1)S(1)} custom-call(f32[32,4,256]{2,1,0:T(4,128)S(1)} %all-to-all-done.refs_1_.info_ref, bf16[32,20,16,128]{3,2,1,0:T(8,128)(2,1)} %get-tuple-element.15.refs_0_, bf16[32,15,16,128]{3,2,1,0:T(8,128)(2,1)S(1)} %get-tuple-element.16.refs_1_, ...), custom_call_target="tpu_custom_call", output_to_operand_aliasing={{}: (2, {})} | custom-call | flops 1342177280 | bytes 6291456 | tf_op jit(solution)/shard_map/gather_obs/pallas_call | solution.py:200
  49.7 10.6 %all-to-all-done.4.x_ref = bf16[32,8,16,128]{3,2,1,0:T(8,128)(2,1)} async-done(((bf16[32,8,16,128]{3,2,1,0:T(8,128)(2,1)}), bf16[32,8,16,128]{3,2,1,0:T(8,128)(2,1)}, u32[]{:S(2)}, u32[]{:S(2)}) %all-to-all-start.4) | async-done | bytes 1048608 | tf_op jit(solution)/shard_map/all_to_all | solution.py:397
  60.3 42.6 %all_to_all.30.own.x_ref = bf16[32,15,16,128]{3,2,1,0:T(8,128)(2,1)} all-to-all(bf16[32,15,16,128]{3,2,1,0:T(8,128)(2,1)S(1)} %gather_obs.1), channel_id=1, replica_groups=mesh['member'=32,'tile'=8] {'member'}, dimensions={0} | all-to-all | bytes 3932160 | tf_op jit(solution)/shard_map/all_to_all | solution.py:397
  102.9 6.3 %all-to-all-start.1 = ((bf16[32,20,16,128]{3,2,1,0:T(8,128)(2,1)}), bf16[32,20,16,128]{3,2,1,0:T(8,128)(2,1)S(1)}, u32[]{:S(2)}, u32[]{:S(2)}) async-start(bf16[32,20,16,128]{3,2,1,0:T(8,128)(2,1)} %get-tuple-element.15.refs_0_), calls=%async_computation.1 | async-start | bytes 5242880 | tf_op jit(solution)/shard_map/all_to_all | solution.py:397
  109.2 1.8 slice.4
  111.0 1.9 collective-permute-start.1
  112.9 2.4 collective-permute-start
  115.4 3.2 %collective-permute-start.3 = (f32[3,4,256]{2,1,0:T(4,128)S(1)}, f32[3,4,256]{2,1,0:T(4,128)S(1)}, u32[]{:S(2)}, u32[]{:S(2)}) collective-permute-start(f32[3,4,256]{2,1,0:T(4,128)S(1)} %pad_maximum_fusion.own_info), channel_id=1, source_target_pairs={{1,0},{2,1},{3,2},{4,3},{5,4},{6,5},{7,6},{9,8},{10,9},{11,10},{12... | collective-permute-start | bytes 36872 | tf_op jit(solution)/shard_map/ppermute | solution.py:423
  118.6 2.1 collective-permute-start.2
  120.7 0.0 collective-permute-done.3.above_info
  120.7 2.9 %collective-permute-done.2.below_info = f32[3,4,256]{2,1,0:T(4,128)S(1)} collective-permute-done((f32[3,4,256]{2,1,0:T(4,128)S(1)}, f32[3,4,256]{2,1,0:T(4,128)S(1)}, u32[]{:S(2)}, u32[]{:S(2)}) %collective-permute-start.2) | collective-permute-done | bytes 12320 | tf_op jit(solution)/shard_map/ppermute | solution.py:423
  123.6 0.0 collective-permute-done.1.above
  123.6 0.0 collective-permute-done.below
  123.6 0.0 copy-start.3
  123.6 0.7 copy-done.3
  124.3 0.0 copy-start.1
  124.3 1.5 copy-done.1
  125.9 0.0 copy-start.4
  125.9 1.0 copy-done.4
  126.9 9.9 %tile_weights.1 = (bf16[2,256,256]{2,1,0:T(8,128)(2,1)S(1)}, f32[2,256,128]{2,1,0:T(8,128)S(1)}) custom-call(bf16[32,15,16,128]{3,2,1,0:T(8,128)(2,1)S(1)} %copy-done.1, bf16[32,3,16,128]{3,2,1,0:T(8,128)(2,1)S(1)} %copy-done.4, bf16[32,3,16,128]{3,2,1,0:T(8,128)(2,1)S(1)} %collective-permute-done.1.above, f32[3,4,256]{2,1,0:T(4,128)S(1)} %pad_maximum_fusion.own_info, ...), custom_call_target="tpu_custom_call" | custom-call | flops 5368709120 | bytes 3145728 | tf_op jit(solution)/shard_map/tile_weights/pallas_call | solution.py:305
  136.8 0.0 copy-start.2
  136.8 3.0 %transform.4.rest_0_ = bf16[32,20,16,128]{3,2,1,0:T(8,128)(2,1)} custom-call(bf16[32,8,16,128]{3,2,1,0:T(8,128)(2,1)} %all-to-all-done.4.x_ref, bf16[2,256,256]{2,1,0:T(8,128)(2,1)S(1)} %get-tuple-element.17.w_ref, f32[2,256,128]{2,1,0:T(8,128)S(1)} %get-tuple-element.18.keep_ref), custom_call_target="tpu_custom_call" | custom-call | flops 268435456 | bytes 2097152 | tf_op jit(solution)/shard_map/transform/pallas_call | solution.py:351
  139.8 0.0 copy-done.2
  139.8 2.8 %transform.5 = bf16[32,20,16,128]{3,2,1,0:T(8,128)(2,1)} custom-call(bf16[32,15,16,128]{3,2,1,0:T(8,128)(2,1)S(1)} %copy-done.2, bf16[2,256,256]{2,1,0:T(8,128)(2,1)S(1)} %get-tuple-element.17.w_ref, f32[2,256,128]{2,1,0:T(8,128)S(1)} %get-tuple-element.18.keep_ref, bf16[32,20,16,128]{3,2,1,0:T(8,128)(2,1)} %transform.4.rest_0_), custom_call_target="tpu_custom_call", output_to_operand_aliasing={{}: (3, {})} | custom-call | flops 402653184 | bytes 3145728 | tf_op jit(solution)/shard_map/transform/pallas_call | solution.py:351
  142.6 16.3 %all-to-all-done.1.x_ref = bf16[32,20,16,128]{3,2,1,0:T(8,128)(2,1)S(1)} async-done(((bf16[32,20,16,128]{3,2,1,0:T(8,128)(2,1)}), bf16[32,20,16,128]{3,2,1,0:T(8,128)(2,1)S(1)}, u32[]{:S(2)}, u32[]{:S(2)}) %all-to-all-start.1) | async-done | bytes 2621472 | tf_op jit(solution)/shard_map/all_to_all | solution.py:397
  158.9 6.9 %all-to-all-start.5 = ((bf16[32,20,16,128]{3,2,1,0:T(8,128)(2,1)}), bf16[32,20,16,128]{3,2,1,0:T(8,128)(2,1)}, u32[]{:S(2)}, u32[]{:S(2)}) async-start(bf16[32,20,16,128]{3,2,1,0:T(8,128)(2,1)} %transform.5), calls=%async_computation.5 | async-start | bytes 5242880 | tf_op jit(solution)/shard_map/all_to_all | solution.py:397
  165.8 2.6 transform.3
  168.4 0.0 copy-start
  168.4 1.5 copy-done
  170.0 45.6 %all-to-all-done.5.x_ref = bf16[32,20,16,128]{3,2,1,0:T(8,128)(2,1)} async-done(((bf16[32,20,16,128]{3,2,1,0:T(8,128)(2,1)}), bf16[32,20,16,128]{3,2,1,0:T(8,128)(2,1)}, u32[]{:S(2)}, u32[]{:S(2)}) %all-to-all-start.5) | async-done | bytes 2621472 | tf_op jit(solution)/shard_map/all_to_all | solution.py:397
  215.6 6.5 %all-to-all-start.3 = ((bf16[32,20,16,128]{3,2,1,0:T(8,128)(2,1)}), bf16[32,20,16,128]{3,2,1,0:T(8,128)(2,1)}, u32[]{:S(2)}, u32[]{:S(2)}) async-start(bf16[32,20,16,128]{3,2,1,0:T(8,128)(2,1)} %copy-done), calls=%async_computation.3 | async-start | bytes 5242880 | tf_op jit(solution)/shard_map/all_to_all | solution.py:397
  222.1 6.9 %unpack.2.rest_0_ = bf16[8,80,8,512]{3,2,1,0:T(8,128)(2,1)} custom-call(bf16[32,20,16,128]{3,2,1,0:T(8,128)(2,1)} %all-to-all-done.5.x_ref), custom_call_target="tpu_custom_call" | custom-call | flops 52428800 | bytes 5242880 | tf_op jit(solution)/shard_map/unpack/pallas_call | solution.py:147
  228.9 42.5 %all-to-all-done.3.x_ref = bf16[32,20,16,128]{3,2,1,0:T(8,128)(2,1)} async-done(((bf16[32,20,16,128]{3,2,1,0:T(8,128)(2,1)}), bf16[32,20,16,128]{3,2,1,0:T(8,128)(2,1)}, u32[]{:S(2)}, u32[]{:S(2)}) %all-to-all-start.3) | async-done | bytes 2621472 | tf_op jit(solution)/shard_map/all_to_all | solution.py:397
  271.4 6.8 %unpack.3 = bf16[8,80,8,512]{3,2,1,0:T(8,128)(2,1)} custom-call(bf16[32,20,16,128]{3,2,1,0:T(8,128)(2,1)} %all-to-all-done.3.x_ref, bf16[8,80,8,512]{3,2,1,0:T(8,128)(2,1)} %unpack.2.rest_0_), custom_call_target="tpu_custom_call", output_to_operand_aliasing={{}: (1, {})} | custom-call | flops 52428800 | bytes 5242880 | tf_op jit(solution)/shard_map/unpack/pallas_call | solution.py:147
  (4 shorter events, 0.0 us)
Async XLA Ops:
  2.1 21.8 %all-to-all-start = ((f32[32,4,256]{2,1,0:T(4,128)}), f32[32,4,256]{2,1,0:T(4,128)S(1)}, u32[]{:S(2)}, u32[]{:S(2)}) async-start(f32[32,4,256]{2,1,0:T(4,128)} %slot_rows.1), calls=%async_computation | async-start | bytes 262144 | tf_op jit(solution)/shard_map/all_to_all | solution.py:397
  37.3 23.0 %all-to-all-start.4 = ((bf16[32,8,16,128]{3,2,1,0:T(8,128)(2,1)}), bf16[32,8,16,128]{3,2,1,0:T(8,128)(2,1)}, u32[]{:S(2)}, u32[]{:S(2)}) async-start(bf16[32,8,16,128]{3,2,1,0:T(8,128)(2,1)} %get-tuple-element.14.refs_2_), calls=%async_computation.4 | async-start | bytes 2097152 | tf_op jit(solution)/shard_map/all_to_all | solution.py:397
  102.9 56.0 %all-to-all-start.1 = ((bf16[32,20,16,128]{3,2,1,0:T(8,128)(2,1)}), bf16[32,20,16,128]{3,2,1,0:T(8,128)(2,1)S(1)}, u32[]{:S(2)}, u32[]{:S(2)}) async-start(bf16[32,20,16,128]{3,2,1,0:T(8,128)(2,1)} %get-tuple-element.15.refs_0_), calls=%async_computation.1 | async-start | bytes 5242880 | tf_op jit(solution)/shard_map/all_to_all | solution.py:397
  111.0 12.6 %collective-permute-start.1 = (bf16[32,3,16,128]{3,2,1,0:T(8,128)(2,1)}, bf16[32,3,16,128]{3,2,1,0:T(8,128)(2,1)S(1)}, u32[]{:S(2)}, u32[]{:S(2)}) collective-permute-start(bf16[32,3,16,128]{3,2,1,0:T(8,128)(2,1)} %slice.4), channel_id=1, source_target_pairs={{1,0},{2,1},{3,2},{4,3},{5,4},{6,5},{7,6},{9,8},{10,9},{11,10},{12... | collective-permute-start | bytes 1179656 | tf_op jit(solution)/shard_map/ppermute | solution.py:422
  112.9 10.7 %collective-permute-start = (bf16[32,3,16,128]{3,2,1,0:T(8,128)(2,1)}, bf16[32,3,16,128]{3,2,1,0:T(8,128)(2,1)S(1)}, u32[]{:S(2)}, u32[]{:S(2)}) collective-permute-start(bf16[32,3,16,128]{3,2,1,0:T(8,128)(2,1)} %slice.4), channel_id=1, source_target_pairs={{0,1},{1,2},{2,3},{3,4},{4,5},{5,6},{6,7},{8,9},{9,10},{10,11},{11... | collective-permute-start | bytes 1179656 | tf_op jit(solution)/shard_map/ppermute | solution.py:422
  115.4 5.3 %collective-permute-start.3 = (f32[3,4,256]{2,1,0:T(4,128)S(1)}, f32[3,4,256]{2,1,0:T(4,128)S(1)}, u32[]{:S(2)}, u32[]{:S(2)}) collective-permute-start(f32[3,4,256]{2,1,0:T(4,128)S(1)} %pad_maximum_fusion.own_info), channel_id=1, source_target_pairs={{1,0},{2,1},{3,2},{4,3},{5,4},{6,5},{7,6},{9,8},{10,9},{11,10},{12... | collective-permute-start | bytes 36872 | tf_op jit(solution)/shard_map/ppermute | solution.py:423
  118.6 5.0 %collective-permute-start.2 = (f32[3,4,256]{2,1,0:T(4,128)S(1)}, f32[3,4,256]{2,1,0:T(4,128)S(1)}, u32[]{:S(2)}, u32[]{:S(2)}) collective-permute-start(f32[3,4,256]{2,1,0:T(4,128)S(1)} %pad_maximum_fusion.own_info), channel_id=1, source_target_pairs={{0,1},{1,2},{2,3},{3,4},{4,5},{5,6},{6,7},{8,9},{9,10},{10,11},{11... | collective-permute-start | bytes 36872 | tf_op jit(solution)/shard_map/ppermute | solution.py:423
  123.6 0.8 copy-start.3
  124.3 1.5 copy-start.1
  125.9 1.0 copy-start.4
  136.8 3.0 %copy-start.2 = (bf16[32,15,16,128]{3,2,1,0:T(8,128)(2,1)S(1)}, bf16[32,15,16,128]{3,2,1,0:T(8,128)(2,1)}, u32[]{:S(2)}) copy-start(bf16[32,15,16,128]{3,2,1,0:T(8,128)(2,1)} %all_to_all.30.own.x_ref) | copy-start | bytes 5898244
  158.9 56.7 %all-to-all-start.5 = ((bf16[32,20,16,128]{3,2,1,0:T(8,128)(2,1)}), bf16[32,20,16,128]{3,2,1,0:T(8,128)(2,1)}, u32[]{:S(2)}, u32[]{:S(2)}) async-start(bf16[32,20,16,128]{3,2,1,0:T(8,128)(2,1)} %transform.5), calls=%async_computation.5 | async-start | bytes 5242880 | tf_op jit(solution)/shard_map/all_to_all | solution.py:397
  168.4 1.5 copy-start
  215.6 55.8 %all-to-all-start.3 = ((bf16[32,20,16,128]{3,2,1,0:T(8,128)(2,1)}), bf16[32,20,16,128]{3,2,1,0:T(8,128)(2,1)}, u32[]{:S(2)}, u32[]{:S(2)}) async-start(bf16[32,20,16,128]{3,2,1,0:T(8,128)(2,1)} %copy-done), calls=%async_computation.3 | async-start | bytes 5242880 | tf_op jit(solution)/shard_map/all_to_all | solution.py:397

commit v6 on v5

--- a/solution.py
+++ b/solution.py
@@ -402,9 +402,12 @@
         slot_rows(obs_count, obs_cell, obs_channel, obs_value, obs_precision)
     )
     parity = (1 - (lax.axis_index("tile") & 1)).astype(jnp.int32).reshape(1)
-    (lead,) = pack(0, parity, background, (2,))
-    lead, *rest = pack(1, parity, background, (2, 0, 1), (lead,), (info,))
-    rest = pack(0, parity, background, (0, 1), tuple(rest), (lead,))
+    lead, middle = pack(0, parity, background, (2, 1))
+    lead, middle, longest = pack(
+        1, parity, background, (2, 1, 0), (lead, middle), (info,)
+    )
+    (longest,) = pack(0, parity, background, (0,), (longest,), (lead,))
+    rest = (longest, middle)
     blocks = [rest[0], rest[1], lead]
     blocks[CARRIER] = gather_obs(info, blocks)
     arrived = [exchange(b) for b in blocks]

time: 280 us -> 282 us (level)
  waiting for transfers between devices: 128 us -> 132 us
    all_to_all x5, waiting for transfers between devices: 125 us -> 129 us  [exchange(): lax.all_to_all(blocks, 'member', split_axis=0, concat_axis=0, tiled=True)]
where the time goes in v6:
time: 282 us; the launch traced here: 281 us
  waiting for transfers between devices  132 us (47%)
  Pallas kernels  54.5 us (19%)
  starting transfers between devices  44.1 us (16%)
  blocking collectives  43.2 us (15%)
  local copies, waits for them, and re-layouts  6.62 us (2%)
    all_to_all x5, waiting for transfers between devices, exchange(): lax.all_to_all(blocks, 'member', split_axis=0, concat_axis=0, tiled=True)  129 us
    all_to_all x1, blocking collectives, exchange(): lax.all_to_all(blocks, 'member', split_axis=0, concat_axis=0, tiled=True)  43.2 us
    all_to_all x5, starting transfers between devices, exchange(): lax.all_to_all(blocks, 'member', split_axis=0, concat_axis=0, tiled=True)  34.5 us
    pallas_call x2, Pallas kernels, unpack(): pl.pallas_call(functools.partial(unpack_kernel, PER_STEP), out_shape=jax....  13.7 us
    pallas_call x3, Pallas kernels, pack(): pl.pallas_call(functools.partial(pack_kernel, turn, ranges), out_shape=tu...  13.5 us
    pallas_call x1, Pallas kernels, tile_weights(): pl.pallas_call(weights_kernel, out_shape=(jax.ShapeDtypeStruct((2, 256, 2...  9.9 us
    pallas_call x3, Pallas kernels, transform(): pl.pallas_call(functools.partial(transform_kernel, per_step), out_shape=j...  8.35 us
    pallas_call x1, Pallas kernels, gather_obs(): pl.pallas_call(functools.partial(gather_kernel, CHUNKS, tiles), out_shape...  7.7 us
  transfers between devices with their start and end apart: 9, of which 6 were waited for; matrix products, arithmetic and copies ran while one was open for 1% of the time, Pallas kernels for 12%

profile of v6, /device:TPU:8, one launch (start us, length us, event | category | flops | bytes accessed | tf_op | source)
XLA Modules:
  0.0 281.2 jit_solution(14517524626739081807)
XLA Ops:
  0.7 1.4 slot_rows.1
  2.1 11.3 %all-to-all-start = ((f32[32,4,256]{2,1,0:T(4,128)}), f32[32,4,256]{2,1,0:T(4,128)S(1)}, u32[]{:S(2)}, u32[]{:S(2)}) async-start(f32[32,4,256]{2,1,0:T(4,128)} %slot_rows.1), calls=%async_computation | async-start | bytes 262144 | tf_op jit(solution)/shard_map/all_to_all | solution.py:397
  13.4 10.4 %all-to-all-done.refs_2_.info_ref = f32[32,4,256]{2,1,0:T(4,128)S(1)} async-done(((f32[32,4,256]{2,1,0:T(4,128)}), f32[32,4,256]{2,1,0:T(4,128)S(1)}, u32[]{:S(2)}, u32[]{:S(2)}) %all-to-all-start) | async-done | bytes 131104 | tf_op jit(solution)/shard_map/all_to_all | solution.py:397
  23.8 13.4 %pack.4 = (bf16[32,8,16,128]{3,2,1,0:T(8,128)(2,1)}, bf16[32,15,16,128]{3,2,1,0:T(8,128)(2,1)S(1)}, bf16[32,20,16,128]{3,2,1,0:T(8,128)(2,1)}) custom-call(s32[1]{0:T(128)} %bitcast.parity_ref, bf16[8,80,8,512]{3,2,1,0:T(8,128)(2,1)} %x_ref.5, bf16[32,8,16,128]{3,2,1,0:T(8,128)(2,1)} %get-tuple-element.12.refs_0_, ...), custom_call_target="tpu_custom_call", output_to_operand_aliasing={{0}: (2, {}), {1}: (3, {})} | custom-call | flops 104857600 | bytes 10485760 | tf_op jit(solution)/shard_map/pack/pallas_call | solution.py:92
  37.3 4.7 %all-to-all-start.4 = ((bf16[32,8,16,128]{3,2,1,0:T(8,128)(2,1)}), bf16[32,8,16,128]{3,2,1,0:T(8,128)(2,1)}, u32[]{:S(2)}, u32[]{:S(2)}) async-start(bf16[32,8,16,128]{3,2,1,0:T(8,128)(2,1)} %get-tuple-element.15.refs_1_.refs_2_), calls=%async_computation.4 | async-start | bytes 2097152 | tf_op jit(solution)/shard_map/all_to_all | solution.py:397
  42.0 7.7 %gather_obs.1 = bf16[32,15,16,128]{3,2,1,0:T(8,128)(2,1)S(1)} custom-call(f32[32,4,256]{2,1,0:T(4,128)S(1)} %all-to-all-done.refs_2_.info_ref, bf16[32,20,16,128]{3,2,1,0:T(8,128)(2,1)} %pack.5.refs_0_, bf16[32,15,16,128]{3,2,1,0:T(8,128)(2,1)S(1)} %get-tuple-element.16.refs_1_, ...), custom_call_target="tpu_custom_call", output_to_operand_aliasing={{}: (2, {})} | custom-call | flops 1342177280 | bytes 6291456 | tf_op jit(solution)/shard_map/gather_obs/pallas_call | solution.py:200
  49.7 11.2 %all-to-all-done.4.x_ref = bf16[32,8,16,128]{3,2,1,0:T(8,128)(2,1)} async-done(((bf16[32,8,16,128]{3,2,1,0:T(8,128)(2,1)}), bf16[32,8,16,128]{3,2,1,0:T(8,128)(2,1)}, u32[]{:S(2)}, u32[]{:S(2)}) %all-to-all-start.4) | async-done | bytes 1048608 | tf_op jit(solution)/shard_map/all_to_all | solution.py:397
  60.9 43.2 %all_to_all.30.own.x_ref = bf16[32,15,16,128]{3,2,1,0:T(8,128)(2,1)} all-to-all(bf16[32,15,16,128]{3,2,1,0:T(8,128)(2,1)S(1)} %gather_obs.1), channel_id=1, replica_groups=mesh['member'=32,'tile'=8] {'member'}, dimensions={0} | all-to-all | bytes 3932160 | tf_op jit(solution)/shard_map/all_to_all | solution.py:397
  104.1 7.5 %all-to-all-start.1 = ((bf16[32,20,16,128]{3,2,1,0:T(8,128)(2,1)}), bf16[32,20,16,128]{3,2,1,0:T(8,128)(2,1)S(1)}, u32[]{:S(2)}, u32[]{:S(2)}) async-start(bf16[32,20,16,128]{3,2,1,0:T(8,128)(2,1)} %pack.5.refs_0_), calls=%async_computation.1 | async-start | bytes 5242880 | tf_op jit(solution)/shard_map/all_to_all | solution.py:397
  111.6 1.8 slice.4
  113.4 1.9 collective-permute-start.1
  115.3 2.4 collective-permute-start
  117.8 3.2 %collective-permute-start.3 = (f32[3,4,256]{2,1,0:T(4,128)S(1)}, f32[3,4,256]{2,1,0:T(4,128)S(1)}, u32[]{:S(2)}, u32[]{:S(2)}) collective-permute-start(f32[3,4,256]{2,1,0:T(4,128)S(1)} %pad_maximum_fusion.own_info), channel_id=1, source_target_pairs={{1,0},{2,1},{3,2},{4,3},{5,4},{6,5},{7,6},{9,8},{10,9},{11,10},{12... | collective-permute-start | bytes 36872 | tf_op jit(solution)/shard_map/ppermute | solution.py:426
  120.9 2.1 collective-permute-start.2
  123.0 0.0 collective-permute-done.3.above_info
  123.0 2.9 %collective-permute-done.2.below_info = f32[3,4,256]{2,1,0:T(4,128)S(1)} collective-permute-done((f32[3,4,256]{2,1,0:T(4,128)S(1)}, f32[3,4,256]{2,1,0:T(4,128)S(1)}, u32[]{:S(2)}, u32[]{:S(2)}) %collective-permute-start.2) | collective-permute-done | bytes 12320 | tf_op jit(solution)/shard_map/ppermute | solution.py:426
  125.9 0.0 collective-permute-done.1.above
  125.9 0.0 collective-permute-done.below
  125.9 0.0 copy-start.3
  125.9 0.7 copy-done.3
  126.7 0.0 copy-start.1
  126.7 1.5 copy-done.1
  128.2 0.0 copy-start.4
  128.2 1.0 copy-done.4
  129.2 9.9 %tile_weights.1 = (bf16[2,256,256]{2,1,0:T(8,128)(2,1)S(1)}, f32[2,256,128]{2,1,0:T(8,128)S(1)}) custom-call(bf16[32,15,16,128]{3,2,1,0:T(8,128)(2,1)S(1)} %copy-done.1, bf16[32,3,16,128]{3,2,1,0:T(8,128)(2,1)S(1)} %copy-done.4, bf16[32,3,16,128]{3,2,1,0:T(8,128)(2,1)S(1)} %collective-permute-done.1.above, f32[3,4,256]{2,1,0:T(4,128)S(1)} %pad_maximum_fusion.own_info, ...), custom_call_target="tpu_custom_call" | custom-call | flops 5368709120 | bytes 3145728 | tf_op jit(solution)/shard_map/tile_weights/pallas_call | solution.py:305
  139.1 0.0 copy-start.2
  139.2 3.0 %transform.4.rest_0_ = bf16[32,20,16,128]{3,2,1,0:T(8,128)(2,1)} custom-call(bf16[32,8,16,128]{3,2,1,0:T(8,128)(2,1)} %all-to-all-done.4.x_ref, bf16[2,256,256]{2,1,0:T(8,128)(2,1)S(1)} %get-tuple-element.17.w_ref, f32[2,256,128]{2,1,0:T(8,128)S(1)} %get-tuple-element.18.keep_ref), custom_call_target="tpu_custom_call" | custom-call | flops 268435456 | bytes 2097152 | tf_op jit(solution)/shard_map/transform/pallas_call | solution.py:351
  142.1 0.0 copy-done.2
  142.1 2.8 transform.5
  144.9 13.0 %all-to-all-done.1.x_ref = bf16[32,20,16,128]{3,2,1,0:T(8,128)(2,1)S(1)} async-done(((bf16[32,20,16,128]{3,2,1,0:T(8,128)(2,1)}), bf16[32,20,16,128]{3,2,1,0:T(8,128)(2,1)S(1)}, u32[]{:S(2)}, u32[]{:S(2)}) %all-to-all-start.1) | async-done | bytes 2621472 | tf_op jit(solution)/shard_map/all_to_all | solution.py:397
  158.0 6.2 %all-to-all-start.5 = ((bf16[32,20,16,128]{3,2,1,0:T(8,128)(2,1)}), bf16[32,20,16,128]{3,2,1,0:T(8,128)(2,1)}, u32[]{:S(2)}, u32[]{:S(2)}) async-start(bf16[32,20,16,128]{3,2,1,0:T(8,128)(2,1)} %transform.5), calls=%async_computation.5 | async-start | bytes 5242880 | tf_op jit(solution)/shard_map/all_to_all | solution.py:397
  164.1 2.6 transform.3
  166.7 0.0 copy-start
  166.7 1.5 copy-done
  168.2 48.5 %all-to-all-done.5.x_ref = bf16[32,20,16,128]{3,2,1,0:T(8,128)(2,1)} async-done(((bf16[32,20,16,128]{3,2,1,0:T(8,128)(2,1)}), bf16[32,20,16,128]{3,2,1,0:T(8,128)(2,1)}, u32[]{:S(2)}, u32[]{:S(2)}) %all-to-all-start.5) | async-done | bytes 2621472 | tf_op jit(solution)/shard_map/all_to_all | solution.py:397
  216.7 4.9 %all-to-all-start.3 = ((bf16[32,20,16,128]{3,2,1,0:T(8,128)(2,1)}), bf16[32,20,16,128]{3,2,1,0:T(8,128)(2,1)}, u32[]{:S(2)}, u32[]{:S(2)}) async-start(bf16[32,20,16,128]{3,2,1,0:T(8,128)(2,1)} %copy-done), calls=%async_computation.3 | async-start | bytes 5242880 | tf_op jit(solution)/shard_map/all_to_all | solution.py:397
  221.6 6.9 %unpack.2.rest_0_ = bf16[8,80,8,512]{3,2,1,0:T(8,128)(2,1)} custom-call(bf16[32,20,16,128]{3,2,1,0:T(8,128)(2,1)} %all-to-all-done.5.x_ref), custom_call_target="tpu_custom_call" | custom-call | flops 52428800 | bytes 5242880 | tf_op jit(solution)/shard_map/unpack/pallas_call | solution.py:147
  228.4 45.9 %all-to-all-done.3.x_ref = bf16[32,20,16,128]{3,2,1,0:T(8,128)(2,1)} async-done(((bf16[32,20,16,128]{3,2,1,0:T(8,128)(2,1)}), bf16[32,20,16,128]{3,2,1,0:T(8,128)(2,1)}, u32[]{:S(2)}, u32[]{:S(2)}) %all-to-all-start.3) | async-done | bytes 2621472 | tf_op jit(solution)/shard_map/all_to_all | solution.py:397
  274.4 6.8 %unpack.3 = bf16[8,80,8,512]{3,2,1,0:T(8,128)(2,1)} custom-call(bf16[32,20,16,128]{3,2,1,0:T(8,128)(2,1)} %all-to-all-done.3.x_ref, bf16[8,80,8,512]{3,2,1,0:T(8,128)(2,1)} %unpack.2.rest_0_), custom_call_target="tpu_custom_call", output_to_operand_aliasing={{}: (1, {})} | custom-call | flops 52428800 | bytes 5242880 | tf_op jit(solution)/shard_map/unpack/pallas_call | solution.py:147
  (4 shorter events, 0.0 us)
Async XLA Ops:
  2.1 21.8 %all-to-all-start = ((f32[32,4,256]{2,1,0:T(4,128)}), f32[32,4,256]{2,1,0:T(4,128)S(1)}, u32[]{:S(2)}, u32[]{:S(2)}) async-start(f32[32,4,256]{2,1,0:T(4,128)} %slot_rows.1), calls=%async_computation | async-start | bytes 262144 | tf_op jit(solution)/shard_map/all_to_all | solution.py:397
  37.3 23.6 %all-to-all-start.4 = ((bf16[32,8,16,128]{3,2,1,0:T(8,128)(2,1)}), bf16[32,8,16,128]{3,2,1,0:T(8,128)(2,1)}, u32[]{:S(2)}, u32[]{:S(2)}) async-start(bf16[32,8,16,128]{3,2,1,0:T(8,128)(2,1)} %get-tuple-element.15.refs_1_.refs_2_), calls=%async_computation.4 | async-start | bytes 2097152 | tf_op jit(solution)/shard_map/all_to_all | solution.py:397
  104.1 53.9 %all-to-all-start.1 = ((bf16[32,20,16,128]{3,2,1,0:T(8,128)(2,1)}), bf16[32,20,16,128]{3,2,1,0:T(8,128)(2,1)S(1)}, u32[]{:S(2)}, u32[]{:S(2)}) async-start(bf16[32,20,16,128]{3,2,1,0:T(8,128)(2,1)} %pack.5.refs_0_), calls=%async_computation.1 | async-start | bytes 5242880 | tf_op jit(solution)/shard_map/all_to_all | solution.py:397
  113.4 12.6 %collective-permute-start.1 = (bf16[32,3,16,128]{3,2,1,0:T(8,128)(2,1)}, bf16[32,3,16,128]{3,2,1,0:T(8,128)(2,1)S(1)}, u32[]{:S(2)}, u32[]{:S(2)}) collective-permute-start(bf16[32,3,16,128]{3,2,1,0:T(8,128)(2,1)} %slice.4), channel_id=1, source_target_pairs={{1,0},{2,1},{3,2},{4,3},{5,4},{6,5},{7,6},{9,8},{10,9},{11,10},{12... | collective-permute-start | bytes 1179656 | tf_op jit(solution)/shard_map/ppermute | solution.py:425
  115.3 10.7 %collective-permute-start = (bf16[32,3,16,128]{3,2,1,0:T(8,128)(2,1)}, bf16[32,3,16,128]{3,2,1,0:T(8,128)(2,1)S(1)}, u32[]{:S(2)}, u32[]{:S(2)}) collective-permute-start(bf16[32,3,16,128]{3,2,1,0:T(8,128)(2,1)} %slice.4), channel_id=1, source_target_pairs={{0,1},{1,2},{2,3},{3,4},{4,5},{5,6},{6,7},{8,9},{9,10},{10,11},{11... | collective-permute-start | bytes 1179656 | tf_op jit(solution)/shard_map/ppermute | solution.py:425
  117.8 5.3 %collective-permute-start.3 = (f32[3,4,256]{2,1,0:T(4,128)S(1)}, f32[3,4,256]{2,1,0:T(4,128)S(1)}, u32[]{:S(2)}, u32[]{:S(2)}) collective-permute-start(f32[3,4,256]{2,1,0:T(4,128)S(1)} %pad_maximum_fusion.own_info), channel_id=1, source_target_pairs={{1,0},{2,1},{3,2},{4,3},{5,4},{6,5},{7,6},{9,8},{10,9},{11,10},{12... | collective-permute-start | bytes 36872 | tf_op jit(solution)/shard_map/ppermute | solution.py:426
  120.9 5.0 %collective-permute-start.2 = (f32[3,4,256]{2,1,0:T(4,128)S(1)}, f32[3,4,256]{2,1,0:T(4,128)S(1)}, u32[]{:S(2)}, u32[]{:S(2)}) collective-permute-start(f32[3,4,256]{2,1,0:T(4,128)S(1)} %pad_maximum_fusion.own_info), channel_id=1, source_target_pairs={{0,1},{1,2},{2,3},{3,4},{4,5},{5,6},{6,7},{8,9},{9,10},{10,11},{11... | collective-permute-start | bytes 36872 | tf_op jit(solution)/shard_map/ppermute | solution.py:426
  125.9 0.8 copy-start.3
  126.7 1.5 copy-start.1
  128.2 1.0 copy-start.4
  139.1 3.0 %copy-start.2 = (bf16[32,15,16,128]{3,2,1,0:T(8,128)(2,1)S(1)}, bf16[32,15,16,128]{3,2,1,0:T(8,128)(2,1)}, u32[]{:S(2)}) copy-start(bf16[32,15,16,128]{3,2,1,0:T(8,128)(2,1)} %all_to_all.30.own.x_ref) | copy-start | bytes 5898244
  158.0 58.8 %all-to-all-start.5 = ((bf16[32,20,16,128]{3,2,1,0:T(8,128)(2,1)}), bf16[32,20,16,128]{3,2,1,0:T(8,128)(2,1)}, u32[]{:S(2)}, u32[]{:S(2)}) async-start(bf16[32,20,16,128]{3,2,1,0:T(8,128)(2,1)} %transform.5), calls=%async_computation.5 | async-start | bytes 5242880 | tf_op jit(solution)/shard_map/all_to_all | solution.py:397
  166.7 1.5 copy-start
  216.7 57.6 %all-to-all-start.3 = ((bf16[32,20,16,128]{3,2,1,0:T(8,128)(2,1)}), bf16[32,20,16,128]{3,2,1,0:T(8,128)(2,1)}, u32[]{:S(2)}, u32[]{:S(2)}) async-start(bf16[32,20,16,128]{3,2,1,0:T(8,128)(2,1)} %copy-done), calls=%async_computation.3 | async-start | bytes 5242880 | tf_op jit(solution)/shard_map/all_to_all | solution.py:397
